TPU v7x, 256 devices: a whole 4x4x8 slice. The times are simulated.
256 devices in a mesh: tile: 32 (over x, z), lev: 8 (over y, core).
Axes of the slice: x: 4, y: 4, z: 8, core: 2. Of those that a mesh axis runs over, the one named last changes fastest.
Arguments:
- tracers: bfloat16 [8192, 4, 64, 128], P('tile', None, 'lev'), may hold values from -6 to 6
- sweeps: bfloat16 [2, 16, 128, 128], replicated, may hold values from -0.2 to 1.2
- targets: int32 [8192, 3], P('tile'), may hold values from 0 to 8191, as said below
- matrix_ids: int32 [8192, 3, 2], P('tile'), may hold values from 0 to 15
- self_ids: int32 [8192, 2], P('tile'), may hold values from 0 to 15
- vertical: float32 [9, 64, 8192], P(None, 'lev', 'tile'), may hold values from -1 to 1
Outputs:
- remapped: bfloat16 [8192, 4, 64, 128], P('tile', None, 'lev')
Inputs may be any that keep to these rules, and one draw needn't show every extreme that they name: `targets`: let the owner of a target be target // 256. There is one hot tile index and one other cold tile index, the same for all sources: the 3 partials of the 256 blocks of every tile index go exactly 48 times to the hot one, never to the cold one, and exactly 24 times to each other tile index.
All inputs are finite; a program needn't handle non-finite values.
Results may differ from a plain program's by a relative error of at most 0.0063.
Values may be sent and summed in bfloat16 or wider, within the bound.
A program may use at most 192 MiB of HBM per device.

v0:
```python
import jax
import jax.numpy as jnp
from jax import lax
from jax.sharding import PartitionSpec as P

REACH = 4


def with_halo(array, sides, width):
    for axis, dim in sides:
        count, length = (lax.axis_size(axis), array.shape[dim])
        up = [(i, (i + 1) % count) for i in range(count - 1)]
        down = [(j, i) for i, j in up]
        last = lax.slice_in_dim(array, length - width, length, axis=dim)
        initial = lax.slice_in_dim(array, 0, width, axis=dim)
        before = lax.ppermute(last, axis, up)
        after = lax.ppermute(initial, axis, down)
        array = jnp.concatenate([before, array, after], axis=dim)
    return array


def sweep_pair(block_rows, sweeps, first_ids, second_ids):
    first_sweep = jnp.einsum(
        "prc,pcd->prd",
        block_rows,
        jnp.take(sweeps[0], first_ids, axis=0),
        preferred_element_type=jnp.float32,
    ).astype(jnp.bfloat16)
    return jnp.einsum(
        "prc,pcd->prd",
        first_sweep,
        jnp.take(sweeps[1], second_ids, axis=0),
        preferred_element_type=jnp.float32,
    )


def on_device(tracers, sweeps, targets, matrix_ids, self_ids, vertical):
    block_count, tracer_count, level_count, cell_count = tracers.shape
    row_count = tracer_count * level_count
    pairs_each = targets.shape[1]
    pair_count = block_count * pairs_each
    blocks = tracers.reshape(block_count, row_count, cell_count)
    tile_count = lax.axis_size("tile")
    share = pair_count // tile_count
    capacity = 2 * share
    slot_count = tile_count * capacity
    order_targets = jnp.transpose(targets).reshape(-1)
    order_ids = jnp.transpose(matrix_ids, (1, 0, 2))
    owner_tile = order_targets // block_count
    owner_hits = (owner_tile[:, None] == jnp.arange(tile_count, dtype=jnp.int32)[None, :]).astype(
        jnp.int32
    )
    before = jnp.sum((jnp.cumsum(owner_hits, axis=0) - owner_hits) * owner_hits, axis=1)
    kept = before < capacity
    pair_numbers = jnp.arange(pair_count, dtype=jnp.int32)
    slot_index = jnp.where(kept, owner_tile * capacity + before, slot_count)
    arrive_index = (
        jnp.full((slot_count,), block_count, jnp.int32)
        .at[slot_index]
        .set(order_targets % block_count, mode="drop")
    )
    slot_pair = jnp.zeros((slot_count,), jnp.int32).at[slot_index].set(pair_numbers, mode="drop")
    own_term = sweep_pair(blocks, sweeps, self_ids[:, 0], self_ids[:, 1])

    def partial_group(pair_ids):
        return sweep_pair(blocks, sweeps, pair_ids[:, 0], pair_ids[:, 1]).astype(jnp.bfloat16)

    partials = lax.map(partial_group, order_ids).reshape(pair_count, row_count, cell_count)
    incoming, arrive_at = (
        lax.all_to_all(partials[slot_pair], "tile", split_axis=0, concat_axis=0, tiled=True),
        lax.all_to_all(arrive_index, "tile", split_axis=0, concat_axis=0, tiled=True),
    )
    received = jax.ops.segment_sum(
        incoming.astype(jnp.float32), arrive_at, num_segments=block_count + 1
    )[:block_count]
    arrived = (
        (own_term + received)
        .astype(jnp.bfloat16)
        .reshape(block_count, tracer_count, level_count, cell_count)
    )
    padded = with_halo(arrived, (("lev", 2),), REACH)
    weights = jnp.transpose(vertical, (0, 2, 1))
    remapped = arrived.astype(jnp.float32)
    for offset in range(2 * REACH + 1):
        remapped = remapped + weights[offset][:, None, :, None] * padded[
            :, :, offset : offset + level_count, :
        ].astype(jnp.float32)
    return remapped.astype(jnp.bfloat16)


def solution(mesh):
    placed = (
        P("tile", None, "lev", None),
        P(),
        P("tile", None),
        P("tile", None, None),
        P("tile", None),
        P(None, "lev", "tile"),
    )
    return jax.shard_map(
        on_device,
        mesh=mesh,
        in_specs=placed,
        out_specs=P("tile", None, "lev", None),
        check_vma=False,
    )
```

profile of v0, /device:TPU:163, one launch (start us, length us, event | category | flops | bytes accessed | tf_op | source)
XLA Modules:
  0.0 699.1 jit_solution(17514223007255582062)
XLA Ops:
  0.0 0.7 reshape.159
  0.7 0.7 reshape.158
  1.4 1.7 reduce-window.6
  3.2 0.3 slice_reduce_fusion
  3.5 0.7 copy.38
  4.2 0.1 fusion.55
  4.3 3.4 scatter_custom_fusion
  7.7 0.7 all_to_all.9
  8.4 8.8 %all-to-all-start = ((s32[32,48,1]{1,2,0:T(1,128)}), s32[32,48,1]{1,2,0:T(1,128)S(1)}, u32[]{:S(2)}, u32[]{:S(2)}) async-start(s32[32,48,1]{1,2,0:T(1,128)} %bitcast.13), calls=%async_computation | async-start | bytes 32768 | tf_op jit(solution)/shard_map/all_to_all | solution.py:71
  17.2 3.4 scatter_custom_fusion.1
  20.6 86.9 %while.10 = (s32[]{:T(128)}, bf16[3,256,32,128]{3,2,1,0:T(8,128)(2,1)}, bf16[2,16,128,128]{3,2,1,0:T(8,128)(2,1)}, s32[3,256,2]{1,2,0:T(2,128)}, bf16[256,32,128]{2,1,0:T(8,128)(2,1)}, /*index=5*/s32[]{:T(128)}) while((s32[]{:T(128)}, bf16[3,256,32,128]{3,2,1,0:T(8,128)(2,1)}, bf16[2,16,128,128]{3,2,1,0:T(8,128)(2,1)}, ...), condition=%wide.region_5.7_spmd, body=%wide.region_4.6_spmd.sunk | while | flops 547363328 | bytes 56651336 | solution.py:68
  20.6 0.7 dynamic-slice_bitcast_fusion.2
  21.3 1.3 slice_bitcast_fusion.14
  22.6 8.6 %gather_fusion = bf16[256,128,128]{2,1,0:T(8,128)(2,1)} fusion(bf16[16,128,128]{2,1,0:T(8,128)(2,1)S(1)} %get-tuple-element.106, s32[1024]{0:T(1024)S(1)} %pad_clamp_fusion.7), kind=kCustom, calls=%fused_computation.1.clone.clone.1 | custom fusion | bytes 16778240 | tf_op jit(solution)/shard_map/while/body/eval_jaxpr/jit(_take)/gather | solution.py:32
  31.2 8.6 %gather_fusion.1 = bf16[256,128,128]{2,1,0:T(8,128)(2,1)} fusion(bf16[16,128,128]{2,1,0:T(8,128)(2,1)S(1)} %get-tuple-element.110, s32[1024]{0:T(1024)S(1)} %pad_clamp_fusion.8), kind=kCustom, calls=%fused_computation.clone.clone.1 | custom fusion | bytes 16778240 | tf_op jit(solution)/shard_map/while/body/eval_jaxpr/jit(_take)/gather | solution.py:26
  39.8 9.8 %bitcast_dynamic-update-slice_fusion.2 = bf16[3,256,32,128]{3,2,1,0:T(8,128)(2,1)} fusion(bf16[3,256,32,128]{3,2,1,0:T(8,128)(2,1)} %get-tuple-element.119, s32[]{:T(128)} %get-tuple-element.118, bf16[256,128,128]{2,1,0:T(8,128)(2,1)} %gather_fusion, pred[256]{0:T(512)(128)(4,1)S(1)} %get-tuple-element.109, ...), kind=kOutput, calls=%fused_computation.16.clone.1 | convolution fusion | flops 547356672 | bytes 20972544 | tf_op jit(solution)/shard_map/while/body/eval_jaxpr/prc,pcd->prd/dot_general | solution.py:29
  49.6 0.7 dynamic-slice_bitcast_fusion.2
  50.3 1.3 slice_bitcast_fusion.14
  51.6 8.6 %gather_fusion = bf16[256,128,128]{2,1,0:T(8,128)(2,1)} fusion(bf16[16,128,128]{2,1,0:T(8,128)(2,1)S(1)} %get-tuple-element.106, s32[1024]{0:T(1024)S(1)} %pad_clamp_fusion.7), kind=kCustom, calls=%fused_computation.1.clone.clone.1 | custom fusion | bytes 16778240 | tf_op jit(solution)/shard_map/while/body/eval_jaxpr/jit(_take)/gather | solution.py:32
  60.2 8.6 %gather_fusion.1 = bf16[256,128,128]{2,1,0:T(8,128)(2,1)} fusion(bf16[16,128,128]{2,1,0:T(8,128)(2,1)S(1)} %get-tuple-element.110, s32[1024]{0:T(1024)S(1)} %pad_clamp_fusion.8), kind=kCustom, calls=%fused_computation.clone.clone.1 | custom fusion | bytes 16778240 | tf_op jit(solution)/shard_map/while/body/eval_jaxpr/jit(_take)/gather | solution.py:26
  68.8 9.7 %bitcast_dynamic-update-slice_fusion.2 = bf16[3,256,32,128]{3,2,1,0:T(8,128)(2,1)} fusion(bf16[3,256,32,128]{3,2,1,0:T(8,128)(2,1)} %get-tuple-element.119, s32[]{:T(128)} %get-tuple-element.118, bf16[256,128,128]{2,1,0:T(8,128)(2,1)} %gather_fusion, pred[256]{0:T(512)(128)(4,1)S(1)} %get-tuple-element.109, ...), kind=kOutput, calls=%fused_computation.16.clone.1 | convolution fusion | flops 547356672 | bytes 20972544 | tf_op jit(solution)/shard_map/while/body/eval_jaxpr/prc,pcd->prd/dot_general | solution.py:29
  78.5 0.7 dynamic-slice_bitcast_fusion.2
  79.2 1.3 slice_bitcast_fusion.14
  80.5 8.6 %gather_fusion = bf16[256,128,128]{2,1,0:T(8,128)(2,1)} fusion(bf16[16,128,128]{2,1,0:T(8,128)(2,1)S(1)} %get-tuple-element.106, s32[1024]{0:T(1024)S(1)} %pad_clamp_fusion.7), kind=kCustom, calls=%fused_computation.1.clone.clone.1 | custom fusion | bytes 16778240 | tf_op jit(solution)/shard_map/while/body/eval_jaxpr/jit(_take)/gather | solution.py:32
  89.1 8.6 %gather_fusion.1 = bf16[256,128,128]{2,1,0:T(8,128)(2,1)} fusion(bf16[16,128,128]{2,1,0:T(8,128)(2,1)S(1)} %get-tuple-element.110, s32[1024]{0:T(1024)S(1)} %pad_clamp_fusion.8), kind=kCustom, calls=%fused_computation.clone.clone.1 | custom fusion | bytes 16778240 | tf_op jit(solution)/shard_map/while/body/eval_jaxpr/jit(_take)/gather | solution.py:26
  97.7 9.8 %bitcast_dynamic-update-slice_fusion.2 = bf16[3,256,32,128]{3,2,1,0:T(8,128)(2,1)} fusion(bf16[3,256,32,128]{3,2,1,0:T(8,128)(2,1)} %get-tuple-element.119, s32[]{:T(128)} %get-tuple-element.118, bf16[256,128,128]{2,1,0:T(8,128)(2,1)} %gather_fusion, pred[256]{0:T(512)(128)(4,1)S(1)} %get-tuple-element.109, ...), kind=kOutput, calls=%fused_computation.16.clone.1 | convolution fusion | flops 547356672 | bytes 20972544 | tf_op jit(solution)/shard_map/while/body/eval_jaxpr/prc,pcd->prd/dot_general | solution.py:29
  107.5 9.7 %gather_fusion.2 = bf16[1536,32,128]{2,1,0:T(8,128)(2,1)} fusion(bf16[768,32,128]{2,1,0:T(8,128)(2,1)} %bitcast.83, s32[2048]{0:T(1024)S(1)} %pad_clamp_fusion.2), kind=kCustom, calls=%fused_computation.4 | custom fusion | bytes 25171968 | tf_op jit(solution)/shard_map/gather | solution.py:70
  117.2 0.0 copy-start.2
  117.2 0.0 copy-start
  117.2 0.0 all-to-all-done
  117.2 9.6 %all-to-all-start.1 = ((bf16[1536,32,128]{2,1,0:T(8,128)(2,1)}), bf16[1536,32,128]{2,1,0:T(8,128)(2,1)}, u32[]{:S(2)}, u32[]{:S(2)}) async-start(bf16[1536,32,128]{2,1,0:T(8,128)(2,1)} %gather_fusion.2), calls=%async_computation.1 | async-start | bytes 25165824 | tf_op jit(solution)/shard_map/all_to_all | solution.py:70
  126.8 0.0 copy-done.2
  126.9 0.0 copy-done
  126.9 0.1 slice_bitcast_fusion.3
  127.0 8.7 %gather_fusion.3 = bf16[256,128,128]{2,1,0:T(8,128)(2,1)} fusion(bf16[16,128,128]{2,1,0:T(8,128)(2,1)S(1)} %get-tuple-element.52, s32[1024]{0:T(1024)S(1)} %pad_clamp_fusion.4), kind=kCustom, calls=%fused_computation.2.clone | custom fusion | bytes 16778240 | tf_op jit(solution)/shard_map/jit(_take)/gather | solution.py:26
  135.7 8.6 %gather_fusion.4 = bf16[256,128,128]{2,1,0:T(8,128)(2,1)} fusion(bf16[16,128,128]{2,1,0:T(8,128)(2,1)S(1)} %get-tuple-element.53, s32[1024]{0:T(1024)S(1)} %pad_clamp_fusion.3), kind=kCustom, calls=%fused_computation.3.clone | custom fusion | bytes 16778240 | tf_op jit(solution)/shard_map/jit(_take)/gather | solution.py:32
  144.3 0.5 broadcast.185
  144.8 0.7 reduce.7
  145.5 0.1 reshape.222
  145.6 285.0 %all-to-all-done.1 = bf16[1536,32,128]{2,1,0:T(8,128)(2,1)} async-done(((bf16[1536,32,128]{2,1,0:T(8,128)(2,1)}), bf16[1536,32,128]{2,1,0:T(8,128)(2,1)}, u32[]{:S(2)}, u32[]{:S(2)}) %all-to-all-start.1) | async-done | bytes 12582944 | tf_op jit(solution)/shard_map/all_to_all | solution.py:70
  430.5 14.5 %convert_element_type.58 = f32[1536,32,128]{2,1,0:T(8,128)} convert(bf16[1536,32,128]{2,1,0:T(8,128)(2,1)} %all-to-all-done.1) | non-fusion elementwise | flops 6291456 | bytes 37748736 | tf_op jit(solution)/shard_map/convert_element_type | solution.py:74
  445.0 2.5 broadcast_in_dim.36
  447.5 207.3 %scatter_fusion = f32[257,32,128]{2,1,0:T(8,128)} fusion(f32[257,32,128]{2,1,0:T(8,128)} %broadcast_in_dim.36, s32[1536]{0:T(1024)S(1)} %reshape.222, f32[1536,32,128]{2,1,0:T(8,128)} %convert_element_type.58), kind=kCustom, calls=%fused_computation.7 | custom fusion | flops 6291456 | bytes 75503616 | tf_op jit(solution)/shard_map/scatter-add | solution.py:73
  654.8 10.0 %fusion.37 = bf16[256,4,8,128]{3,2,1,0:T(8,128)(2,1)S(1)} fusion(f32[257,32,128]{2,1,0:T(8,128)} %scatter_fusion, bf16[256,128,128]{2,1,0:T(8,128)(2,1)} %gather_fusion.4, pred[256]{0:T(512)(128)(4,1)S(1)} %get-tuple-element.67, bf16[256,128,128]{2,1,0:T(8,128)(2,1)} %gather_fusion.3, pred[256]{0:T(512)(128)(4,1)S(1)} %get-tuple-element.68, ...), kind=kOutput, calls=%fused_computation.61 | convolution fusion | flops 548405248 | bytes 25166336 | tf_op jit(solution)/shard_map/prc,pcd->prd/dot_general | solution.py:29
  664.9 0.0 copy-start.1
  664.9 2.0 fusion.71
  666.9 3.6 collective-permute-start
  670.5 1.9 collective-permute-start.1
  672.4 0.0 copy-done.1
  672.4 0.6 slice_bitcast_fusion.12
  673.0 0.1 copy.28
  673.2 0.1 copy.29
  673.3 0.8 copy.30
  674.1 1.5 copy.31
  675.6 1.5 copy.32
  677.1 1.5 copy.33
  678.6 1.5 copy.34
  680.1 0.8 copy.35
  680.8 0.8 copy.36
  681.6 0.9 collective-permute-done
  682.5 4.4 collective-permute-done.1
  686.9 12.0 %fusion.33 = bf16[256,4,8,128]{3,2,1,0:T(8,128)(2,1)} fusion(bf16[256,4,8,128]{3,2,1,0:T(8,128)(2,1)S(1)} %fusion.37, bf16[256,4,4,128]{3,2,1,0:T(4,128)(2,1)} %collective-permute-done.1, bf16[256,4,4,128]{3,2,1,0:T(4,128)(2,1)S(1)} %collective-permute-done, f32[256,8]{1,0:T(8,128)} %copy.36, f32[256,8]{1,0:T(8,128)} %copy.35, f32[256,8]{1,0:T(8,128)} %copy.34, ...), kind=kLoop, calls=%fused_computation.56 | loop fusion | flops 54525952 | bytes 6365184 | tf_op jit(solution)/shard_map/convert_element_type | solution.py:88
  (33 shorter events, 0.3 us)
Async XLA Ops:
  8.4 108.8 %all-to-all-start = ((s32[32,48,1]{1,2,0:T(1,128)}), s32[32,48,1]{1,2,0:T(1,128)S(1)}, u32[]{:S(2)}, u32[]{:S(2)}) async-start(s32[32,48,1]{1,2,0:T(1,128)} %bitcast.13), calls=%async_computation | async-start | bytes 32768 | tf_op jit(solution)/shard_map/all_to_all | solution.py:71
  117.2 9.6 %copy-start.2 = (s32[256,2]{0,1:T(2,128)S(1)}, s32[256,2]{0,1:T(2,128)}, u32[]{:S(2)}) copy-start(s32[256,2]{0,1:T(2,128)} %param.14) | copy-start | bytes 6148
  117.2 9.7 %copy-start = (bf16[2,16,128,128]{3,2,1,0:T(8,128)(2,1)S(1)}, bf16[2,16,128,128]{3,2,1,0:T(8,128)(2,1)}, u32[]{:S(2)}) copy-start(bf16[2,16,128,128]{3,2,1,0:T(8,128)(2,1)} %get-tuple-element.132) | copy-start | bytes 3145732
  117.2 313.3 %all-to-all-start.1 = ((bf16[1536,32,128]{2,1,0:T(8,128)(2,1)}), bf16[1536,32,128]{2,1,0:T(8,128)(2,1)}, u32[]{:S(2)}, u32[]{:S(2)}) async-start(bf16[1536,32,128]{2,1,0:T(8,128)(2,1)} %gather_fusion.2), calls=%async_computation.1 | async-start | bytes 25165824 | tf_op jit(solution)/shard_map/all_to_all | solution.py:70
  664.9 7.5 %copy-start.1 = (f32[9,8,256]{2,1,0:T(8,128)S(1)}, f32[9,8,256]{2,1,0:T(8,128)}, u32[]{:S(2)}) copy-start(f32[9,8,256]{2,1,0:T(8,128)} %param.15) | copy-start | bytes 221188
  666.9 15.6 %collective-permute-start = (bf16[256,4,4,128]{3,2,1,0:T(4,128)(2,1)}, bf16[256,4,4,128]{3,2,1,0:T(4,128)(2,1)S(1)}, u32[]{:S(2)}, u32[]{:S(2)}) collective-permute-start(bf16[256,4,4,128]{3,2,1,0:T(4,128)(2,1)} %get-tuple-element.50), channel_id=1, source_target_pairs={{0,1},{1,2},{2,3},{3,4},{4,5},{5,6},{6,7},{8,9},{9,10},{10,11},{11... | collective-permute-start | bytes 3145736 | tf_op jit(solution)/shard_map/ppermute | solution.py:16
  670.5 16.4 %collective-permute-start.1 = (bf16[256,4,4,128]{3,2,1,0:T(4,128)(2,1)}, bf16[256,4,4,128]{3,2,1,0:T(4,128)(2,1)}, u32[]{:S(2)}, u32[]{:S(2)}) collective-permute-start(bf16[256,4,4,128]{3,2,1,0:T(4,128)(2,1)} %get-tuple-element.51), channel_id=1, source_target_pairs={{1,0},{2,1},{3,2},{4,3},{5,4},{6,5},{7,6},{9,8},{10,9},{11,10},{12... | collective-permute-start | bytes 3145736 | tf_op jit(solution)/shard_map/ppermute | solution.py:17
where the time goes:
time: 703 us; the launch traced here: 699 us
  waiting for transfers between devices  290 us (41%)
  other arithmetic  237 us (34%)
  local copies, waits for them, and re-layouts  109 us (16%)
  matrix products  39.3 us (6%)
  starting transfers between devices  23.9 us (3%)
    all_to_all x1, waiting for transfers between devices, on_device(): lax.all_to_all(partials[slot_pair], 'tile', split_axis=0, concat_axis=0,...  285 us
    scatter-add x1, other arithmetic, on_device(): jax.ops.segment_sum(incoming.astype(jnp.float32), arrive_at, num_segments...  207 us
    dot_general x4, matrix products, sweep_pair(): jnp.einsum('prc,pcd->prd', first_sweep, jnp.take(sweeps[1], second_ids, a...  39.3 us
    gather x4, local copies, waits for them, and re-layouts, sweep_pair(): jnp.take(sweeps[0], first_ids, axis=0)  34.4 us
    gather x4, local copies, waits for them, and re-layouts, sweep_pair(): jnp.take(sweeps[1], second_ids, axis=0)  34.3 us
    convert_element_type x1, other arithmetic, on_device(): incoming.astype(jnp.float32)  14.5 us
  transfers between devices with their start and end apart: 4, of which 3 were waited for; matrix products, arithmetic and copies ran while one was open for 18% of the time, Pallas kernels for 0%

commit v1 on v0

v1 whole, which is shorter than its diff:
```python
import functools

import jax
import jax.numpy as jnp
from jax import lax
from jax.experimental import pallas as pl
from jax.experimental.pallas import tpu as pltpu
from jax.sharding import PartitionSpec as P

MESH = pl.DeviceIdType.MESH
REACH = 4
XN, ZN = 4, 8
TILES = XN * ZN
BLOCKS = 256
CELLS = 128
TRACERS = 4
LEVS = 8
ROWS = TRACERS * LEVS
SHARE = 24
TAP = 2 * REACH + 1
HEAD = 16
PART = SHARE * LEVS
MSG = HEAD + TRACERS * PART
HALF = 384
PITCH = BLOCKS + 8
SLOTS = TILES * SHARE
f32, bf16, i32 = jnp.float32, jnp.bfloat16, jnp.int32


def dot(a, b):
    return jnp.dot(a, b, preferred_element_type=f32)


def plan_kernel(ids_ref, table_ref, index_ref):
    me = lax.axis_index("tile")
    lane = lax.broadcasted_iota(i32, (BLOCKS, 128), 1)
    sub = lax.broadcasted_iota(i32, (BLOCKS, 128), 0)
    before = (
        lax.broadcasted_iota(i32, (BLOCKS, BLOCKS), 1) < lax.broadcasted_iota(i32, (BLOCKS, BLOCKS), 0)
    ).astype(f32).astype(bf16)
    ids = ids_ref[...]
    base = jnp.zeros((1, 128), f32)
    here = None
    total = None
    for j in range(3):
        target = ids[:, j : j + 1]
        apart = ((target >> 8) - me) & (TILES - 1)
        hits = (jnp.broadcast_to(apart, (BLOCKS, 128)) == lane).astype(f32)
        earlier = dot(before, hits.astype(bf16)) + base
        rank = jnp.sum(hits * earlier, axis=1, keepdims=True).astype(i32)
        base = base + jnp.sum(hits, axis=0, keepdims=True)
        extra = rank >= SHARE
        row = jnp.where(extra, TILES, apart)
        entry = jnp.where(extra, rank - SHARE, rank)
        order = jnp.where(extra, me, apart) * SHARE + entry
        chosen = (jnp.broadcast_to(row, (BLOCKS, 128)) == lane).astype(f32)
        at_entry = (jnp.broadcast_to(entry, (BLOCKS, 128)) == lane).astype(f32)
        values = [
            at_entry * sub.astype(f32),
            at_entry * ids[:, 3 + 2 * j : 4 + 2 * j].astype(f32),
            at_entry * ids[:, 4 + 2 * j : 5 + 2 * j].astype(f32),
        ]
        arrival = ((target & (BLOCKS - 1)) + 1).astype(f32)
        for m in range(SLOTS // 128):
            at = (jnp.broadcast_to(order, (BLOCKS, 128)) == lane + 128 * m).astype(f32)
            values.append(at * arrival)
        part = dot(chosen.T.astype(bf16), jnp.concatenate(values, axis=1).astype(bf16))
        total = part if total is None else total + part
    total = total[:40]
    packed = total[:, :128] + 256.0 * total[:, 128:256] + 4096.0 * total[:, 256:384]
    table_ref[...] = packed.astype(i32)
    index_ref[...] = jnp.zeros_like(index_ref)
    for m in range(SLOTS // 128):
        index_ref[:, m, :] = total[:, 384 + 128 * m : 512 + 128 * m]
    index_ref[39] = jnp.broadcast_to((base[:, :1] > SHARE).astype(f32), (8, 128))


def main_kernel(
    table_ref, self_ref, tracers_ref, sweeps_ref, index_ref, vertical_ref, out_ref,
    stage, sbuf, rbuf, ebuf, own, chosen, pad, turned, weight, obuf,
    send_sem, recv_sem, ring_send, ring_recv, cross_send, cross_recv, halo_send, halo_recv, local_sem, out_sem,
):
    me = lax.axis_index("tile")
    lev = lax.axis_index("lev")
    x, z = me // ZN, me % ZN

    def tile_at(dx, dz):
        return ((x + dx + XN) % XN) * ZN + (z + dz + ZN) % ZN

    barrier = pltpu.get_barrier_semaphore()

    def greet(k, carry):
        pl.semaphore_signal(barrier, inc=1, device_id=((me + k) % TILES, lev), device_id_type=MESH)
        return carry

    lax.fori_loop(1, TILES, greet, 0)
    above, below = (lev + 1) % LEVS, (lev + LEVS - 1) % LEVS
    for other in (above, below):
        pl.semaphore_signal(barrier, inc=1, device_id=(me, other), device_id_type=MESH)

    def swept(block, first, second):
        half = dot(tracers_ref[block], sweeps_ref[first]).astype(bf16)
        return dot(half, sweeps_ref[16 + second])

    def build(k):
        for e in range(SHARE):
            v = table_ref[k, e]
            stage[pl.ds(e, ROWS, stride=SHARE), :] = swept(v & 255, (v >> 8) & 15, (v >> 12) & 15)
        sbuf[k, 0:HEAD] = jnp.concatenate([index_ref[k], jnp.zeros((8, 128), f32)], axis=0).astype(bf16)
        for t in range(TRACERS):
            sbuf[k, HEAD + t * PART : HEAD + (t + 1) * PART] = stage[t * PART : (t + 1) * PART, :].astype(bf16)

    def span(t):
        return pl.ds(0, HEAD + PART) if t == 0 else pl.ds(HEAD + t * PART, PART)

    def send(t, k):
        return pltpu.make_async_remote_copy(
            src_ref=sbuf.at[k, span(t)], dst_ref=rbuf.at[k, span(t)],
            send_sem=send_sem.at[t], recv_sem=recv_sem.at[t],
            device_id=((me + k) % TILES, lev), device_id_type=MESH,
        )

    def wait_bytes(buf, t, sem):
        ref = buf.at[pl.ds(1, TILES - 1), span(t)]
        pltpu.make_async_copy(ref, ref, sem).wait()

    def ring(j, way):
        item = x * ZN + (z - way * j + ZN) % ZN
        rows = pl.ds(0, MSG) if j < 3 else (pl.ds(0, HALF) if way > 0 else pl.ds(HALF, MSG - HALF))
        d = 0 if way > 0 else 1
        return pltpu.make_async_remote_copy(
            src_ref=sbuf.at[TILES, rows] if j == 0 else ebuf.at[item, rows],
            dst_ref=ebuf.at[item, rows],
            send_sem=ring_send.at[d, j], recv_sem=ring_recv.at[d, j],
            device_id=(tile_at(0, way), lev), device_id_type=MESH,
        )

    def cross(dx):
        group = pl.ds(x * ZN, ZN)
        return pltpu.make_async_remote_copy(
            src_ref=ebuf.at[group], dst_ref=ebuf.at[group],
            send_sem=cross_send.at[dx - 1], recv_sem=cross_recv.at[dx - 1],
            device_id=(tile_at(dx, 0), lev), device_id_type=MESH,
        )

    def keep(src, dst, i):
        return pltpu.make_async_copy(src, dst, local_sem.at[i])

    keep_extra = keep(sbuf.at[TILES], ebuf.at[me], 0)
    keep_main = keep(sbuf.at[0], rbuf.at[0], 1)
    stops = (7, 13, 19, 25)

    def step(i, carry):
        k = jnp.where(i == 0, TILES, jnp.where(i == TILES, 0, i))
        build(k)

        @pl.when(i == 0)
        def _():
            pl.semaphore_wait(barrier, TILES + 1)
            ring(0, 1).start()
            ring(0, -1).start()
            keep_extra.start()

        @pl.when(jnp.logical_and(i > 0, i < TILES))
        def _():
            send(0, k).start()

        for j, stop in enumerate(stops):
            @pl.when(i == stop)
            def _():
                for way in (1, -1):
                    ring(j, way).wait_recv()
                if j == 0:
                    keep_extra.wait()
                if j < 3:
                    for way in (1, -1):
                        ring(j + 1, way).start()
                else:
                    for dx in (1, 3, 2):
                        cross(dx).start()

        return carry

    lax.fori_loop(0, TILES + 1, step, 0)
    keep_main.start()

    def send_phase(t):
        def one(k, carry):
            send(t, k).start()
            return carry

        lax.fori_loop(1, TILES, one, 0)

    send_phase(1)

    def own_step(g, carry):
        for u in range(8):
            b = g * 8 + u
            v = self_ref[b]
            own[pl.ds(b, ROWS, stride=PITCH), :] = swept(b, v & 15, (v >> 4) & 15)
        return carry

    lax.fori_loop(0, BLOCKS // 8, own_step, 0)

    tap_row = lax.broadcasted_iota(i32, (TAP * LEVS, BLOCKS), 0)
    source = lev * LEVS + tap_row % LEVS + tap_row // LEVS - REACH
    plain = vertical_ref[...] + jnp.where(tap_row // LEVS == REACH, 1.0, 0.0)
    turned[:, : TAP * LEVS] = jnp.where(jnp.logical_and(source >= 0, source < LEVS * LEVS), plain, 0.0).T

    def spread(g, carry):
        rows = pl.ds(pl.multiple_of(g * 8, 8), 8)
        columns = turned[rows, :]
        for n in range(TAP * LEVS):
            weight[n, rows] = jnp.broadcast_to(columns[:, n : n + 1], (8, CELLS))
        return carry

    lax.fori_loop(0, BLOCKS // 8, spread, 0)

    def choose(buf, first, hot):
        def add(s, tile):
            return tile + buf[s, 0:HEAD].astype(f32)

        tile = lax.fori_loop(0, TILES, add, jnp.zeros((HEAD, 128), f32))
        block = lax.broadcasted_iota(i32, (BLOCKS, 128), 0).astype(f32) + 1.0
        for m in range(SLOTS // 128):
            row = tile[m : m + 1]
            if hot is not None:
                row = row * hot
            hit = (jnp.broadcast_to(row, (BLOCKS, 128)) == block).astype(f32)
            chosen[:, first + 128 * m : first + 128 * (m + 1)] = hit.astype(bf16)

    def gather_sum(t):
        def pair(q, carry):
            rows = pl.ds(pl.multiple_of(HEAD + t * PART + q * 2 * SHARE, 16), 2 * SHARE)
            pieces = [buf[s, rows].astype(f32) for buf in (rbuf, ebuf) for s in range(TILES)]
            even = jnp.concatenate([p[:SHARE] for p in pieces], axis=0).astype(bf16)
            odd = jnp.concatenate([p[SHARE:] for p in pieces], axis=0).astype(bf16)
            both = dot(chosen[...], jnp.concatenate([even, odd], axis=1))
            for h in range(2):
                r = t * LEVS + 2 * q + h
                mine = own[pl.ds(pl.multiple_of(r * PITCH, 8), BLOCKS), :]
                pad[t, REACH + 2 * q + h] = (mine + both[:, h * CELLS : (h + 1) * CELLS]).astype(bf16)
            return carry

        lax.fori_loop(0, LEVS // 2, pair, 0)

    def halo(t, way):
        inner = pl.ds(LEVS, REACH) if way > 0 else pl.ds(REACH, REACH)
        outer = pl.ds(0, REACH) if way > 0 else pl.ds(LEVS + REACH, REACH)
        d = 0 if way > 0 else 1
        return pltpu.make_async_remote_copy(
            src_ref=pad.at[t, inner], dst_ref=pad.at[t, outer],
            send_sem=halo_send.at[d, t], recv_sem=halo_recv.at[d, t],
            device_id=(me, above if way > 0 else below), device_id_type=MESH,
        )

    def write_out(t):
        span_out = pl.ds(t * LEVS, LEVS)
        return pltpu.make_async_copy(obuf.at[span_out], out_ref.at[span_out], out_sem.at[t])

    def remap(t):
        def chunk(g, carry):
            rows = pl.ds(pl.multiple_of(g * 16, 16), 16)
            levels = [pad[t, m, rows].astype(f32) for m in range(LEVS + 2 * REACH)]
            for l in range(LEVS):
                total = weight[l, rows] * levels[l]
                for n in range(1, TAP):
                    total = total + weight[n * LEVS + l, rows] * levels[l + n]
                obuf[t * LEVS + l, rows] = total.astype(bf16)
            return carry

        lax.fori_loop(0, BLOCKS // 16, chunk, 0)
        write_out(t).start()

    def finish(t):
        for way in (1, -1):
            halo(t, way).wait_recv()
        remap(t)

    keep_main.wait()
    for t in range(TRACERS):
        wait_bytes(sbuf, t, send_sem.at[t])
        if t + 2 < TRACERS:
            send_phase(t + 2)
        wait_bytes(rbuf, t, recv_sem.at[t])
        if t == 0:
            for dx in (1, 2, 3):
                cross(dx).wait_recv()
            choose(rbuf, 0, None)
            choose(ebuf, SLOTS, index_ref[39][0:1])
        gather_sum(t)
        for way in (1, -1):
            halo(t, way).start()
        if t > 0:
            finish(t - 1)
    finish(TRACERS - 1)
    for t in range(TRACERS):
        write_out(t).wait()
        for way in (1, -1):
            halo(t, way).wait_send()
    for j in range(4):
        for way in (1, -1):
            ring(j, way).wait_send()
    for dx in (1, 2, 3):
        cross(dx).wait_send()


def on_device(tracers, sweeps, targets, matrix_ids, self_ids, vertical):
    vmem = pl.BlockSpec(memory_space=pltpu.VMEM)
    smem = pl.BlockSpec(memory_space=pltpu.SMEM)
    ids = jnp.concatenate([targets, matrix_ids.reshape(BLOCKS, 6)], axis=1)
    table, index = pl.pallas_call(
        plan_kernel,
        name="plan",
        out_shape=(jax.ShapeDtypeStruct((40, 128), i32), jax.ShapeDtypeStruct((40, 8, 128), f32)),
        in_specs=[vmem],
        out_specs=(vmem, vmem),
    )(ids)
    own_ids = self_ids[:, 0] + 16 * self_ids[:, 1]
    dma = pltpu.SemaphoreType.DMA
    out = pl.pallas_call(
        main_kernel,
        name="remap",
        out_shape=jax.ShapeDtypeStruct((ROWS, BLOCKS, CELLS), bf16),
        in_specs=[smem, smem, vmem, vmem, vmem, vmem],
        out_specs=pl.BlockSpec(memory_space=pl.ANY),
        scratch_shapes=[
            pltpu.VMEM((SHARE * ROWS, CELLS), f32),
            pltpu.VMEM((TILES + 1, MSG, CELLS), bf16),
            pltpu.VMEM((TILES, MSG, CELLS), bf16),
            pltpu.VMEM((TILES, MSG, CELLS), bf16),
            pltpu.VMEM((ROWS * PITCH, CELLS), f32),
            pltpu.VMEM((BLOCKS, 2 * SLOTS), bf16),
            pltpu.VMEM((TRACERS, LEVS + 2 * REACH, BLOCKS, CELLS), bf16),
            pltpu.VMEM((BLOCKS, 128), f32),
            pltpu.VMEM((TAP * LEVS, BLOCKS, CELLS), f32),
            pltpu.VMEM((ROWS, BLOCKS, CELLS), bf16),
            dma((TRACERS,)), dma((TRACERS,)), dma((2, 4)), dma((2, 4)), dma((3,)), dma((3,)),
            dma((2, TRACERS)), dma((2, TRACERS)), dma((2,)), dma((TRACERS,)),
        ],
        compiler_params=pltpu.CompilerParams(
            collective_id=0, has_side_effects=True, vmem_limit_bytes=56 * 1024 * 1024
        ),
    )(
        table,
        own_ids,
        tracers.reshape(BLOCKS, ROWS, CELLS),
        sweeps.reshape(-1, CELLS, CELLS),
        index,
        vertical.reshape(TAP * LEVS, BLOCKS),
    )
    return jnp.transpose(out, (1, 0, 2)).reshape(BLOCKS, TRACERS, LEVS, CELLS)


def solution(mesh):
    placed = (
        P("tile", None, "lev", None),
        P(),
        P("tile", None),
        P("tile", None, None),
        P("tile", None),
        P(None, "lev", "tile"),
    )
    return jax.shard_map(
        on_device,
        mesh=mesh,
        in_specs=placed,
        out_specs=P("tile", None, "lev", None),
        check_vma=False,
    )
```

time: 703 us -> 220 us (0.31)
  the two profiles are of different devices: /device:TPU:163 before, /device:TPU:1 now
where the time goes in v1:
time: 220 us; the launch traced here: 216 us
  Pallas kernels  208 us (95%)
  local copies, waits for them, and re-layouts  5.73 us (3%)
    pallas_call x1, Pallas kernels, on_device(): pl.pallas_call(main_kernel, name='remap', out_shape=jax.ShapeDtypeStruct(...  205 us

profile of v1, /device:TPU:1, one launch (start us, length us, event | category | flops | bytes accessed | tf_op | source)
XLA Modules:
  0.0 216.0 jit_solution(10127000744958574321)
XLA Ops:
  0.0 1.3 multiply_add_fusion
  1.3 0.7 reshape.18
  2.0 0.7 pad_add_fusion
  2.7 0.8 copy.13.ids_ref
  3.4 3.4 %plan.1 = (s32[40,128]{1,0:T(8,128)}, f32[40,8,128]{2,1,0:T(8,128)}) custom-call(s32[256,9]{1,0:T(8,128)} %copy.13.ids_ref), custom_call_target="tpu_custom_call" | custom-call | tf_op jit(solution)/shard_map/plan/pallas_call | solution.py:312
  6.9 204.9 %remap.1 = bf16[32,256,128]{2,1,0:T(8,128)(2,1)} custom-call(s32[40,128]{1,0:T(8,128)} %get-tuple-element.7.table_ref, s32[256]{0:T(256)} %bitcast.13, bf16[256,32,128]{2,1,0:T(8,128)(2,1)} %bitcast.10, bf16[32,128,128]{2,1,0:T(8,128)(2,1)} %bitcast.11, f32[40,8,128]{2,1,0:T(8,128)} %get-tuple-element.8.index_ref, f32[72,256]{1,0:T(8,128)} %bitcast.12), custom_call_target="tpu_custom_call" | custom-call | tf_op jit(solution)/shard_map/remap/pallas_call | solution.py:321
  211.8 4.3 %copy.14 = bf16[256,4,8,128]{3,2,1,0:T(8,128)(2,1)} copy(bf16[256,4,8,128]{3,0,2,1:T(8,128)(2,1)} %bitcast.9) | data formatting | bytes 4194304 | tf_op jit(solution)/shard_map/reshape | solution.py:352

commit v2 on v1

v2 whole, which is shorter than its diff:
```python
import functools

import jax
import jax.numpy as jnp
from jax import lax
from jax.experimental import pallas as pl
from jax.experimental.pallas import tpu as pltpu
from jax.sharding import PartitionSpec as P

MESH = pl.DeviceIdType.MESH
REACH = 4
XN, ZN = 4, 8
TILES = XN * ZN
BLOCKS = 256
CELLS = 128
TRACERS = 4
LEVS = 8
ROWS = TRACERS * LEVS
SHARE = 24
TAP = 2 * REACH + 1
HEAD = 16
PART = SHARE * LEVS
MSG = HEAD + TRACERS * PART
HALF = 384
PITCH = BLOCKS + 8
SLOTS = TILES * SHARE
STOPS = (5, 10, 15, 20)
f32, bf16, i32 = jnp.float32, jnp.bfloat16, jnp.int32


def dot(a, b):
    return jnp.dot(a, b, preferred_element_type=f32)


def main_kernel(
    target_ref, matrix_ref, self_ref, tracers_in, sweeps_in, vertical_in, out_ref,
    tracers_ref, sweeps_ref, vertical_ref, table_made, table_ref, index_ref,
    stage, sbuf, rbuf, ebuf, own, chosen, pad, turned, weight, turn, obuf,
    in_sem, send_sem, recv_sem, ring_send, ring_recv, cross_send, cross_recv, halo_send, halo_recv, local_sem, out_sem,
):
    me = lax.axis_index("tile")
    lev = lax.axis_index("lev")
    x, z = me // ZN, me % ZN

    def tile_at(dx, dz):
        return ((x + dx + XN) % XN) * ZN + (z + dz + ZN) % ZN

    def tile_of(k):
        return tile_at(k // ZN, k % ZN)

    loads = [
        pltpu.make_async_copy(src, dst, in_sem.at[n])
        for n, (src, dst) in enumerate(
            ((sweeps_in, sweeps_ref), (tracers_in, tracers_ref), (vertical_in, vertical_ref))
        )
    ]
    for load in loads:
        load.start()
    barrier = pltpu.get_barrier_semaphore()

    def greet(k, carry):
        pl.semaphore_signal(barrier, inc=1, device_id=(tile_of(k), lev), device_id_type=MESH)
        return carry

    lax.fori_loop(1, TILES, greet, 0)
    above, below = (lev + 1) % LEVS, (lev + LEVS - 1) % LEVS
    for other in (above, below):
        pl.semaphore_signal(barrier, inc=1, device_id=(me, other), device_id_type=MESH)

    def plan():
        sub = lax.broadcasted_iota(i32, (40, BLOCKS), 0)
        slot = lax.broadcasted_iota(i32, (SLOTS, BLOCKS), 0)
        block = lax.broadcasted_iota(i32, (1, BLOCKS), 1).astype(f32)
        before = (
            lax.broadcasted_iota(i32, (BLOCKS, BLOCKS), 0) < lax.broadcasted_iota(i32, (BLOCKS, BLOCKS), 1)
        ).astype(f32).astype(bf16)
        base = jnp.zeros((40, 1), f32)
        total = None
        for j in range(3):
            target = target_ref[j : j + 1, :]
            owner = target >> 8
            apart = (((owner >> 3) - x) & (XN - 1)) * ZN + (((owner & (ZN - 1)) - z) & (ZN - 1))
            hits = (jnp.broadcast_to(apart, (40, BLOCKS)) == sub).astype(f32)
            earlier = dot(hits.astype(bf16), before) + base
            rank = jnp.sum(hits * earlier, axis=0, keepdims=True).astype(i32)
            base = base + jnp.sum(hits, axis=1, keepdims=True)
            extra = rank >= SHARE
            row = jnp.where(extra, TILES, apart)
            entry = jnp.where(extra, rank - SHARE, rank)
            order = jnp.where(extra, me, apart) * SHARE + entry
            taken = (jnp.broadcast_to(row, (40, BLOCKS)) == sub).astype(f32).astype(bf16)
            at_entry = (jnp.broadcast_to(entry, (32, BLOCKS)) == sub[:32]).astype(f32)
            arrival = ((target & (BLOCKS - 1)) + 1).astype(f32)
            ids = matrix_ref[j].astype(f32)
            at = (jnp.broadcast_to(order, (SLOTS, BLOCKS)) == slot).astype(f32)
            values = jnp.concatenate(
                [at_entry * block, at_entry * ids[0:1], at_entry * ids[1:2], at_entry, at * arrival], axis=0
            ).astype(bf16)
            part = lax.dot_general(taken, values, (((1,), (1,)), ((), ())), preferred_element_type=f32)
            total = part if total is None else total + part
        table_made[...] = total[:, :128].astype(i32)
        for m in range(SLOTS // 128):
            index_ref[:, m, :] = total[:, 128 * (m + 1) : 128 * (m + 2)]
        for m in range(SLOTS // 128, 8):
            index_ref[:, m, :] = jnp.zeros((40, 128), f32)
        index_ref[39] = jnp.broadcast_to((base[0:1] > SHARE).astype(f32), (8, 128))
        copy = pltpu.make_async_copy(table_made, table_ref, in_sem.at[3])
        copy.start()
        copy.wait()

    plan()
    for load in loads:
        load.wait()

    def swept(block, first, second):
        half = dot(tracers_ref[block], sweeps_ref[first]).astype(bf16)
        return dot(half, sweeps_ref[16 + second])

    def build(k):
        for e in range(SHARE):
            stage[pl.ds(e, ROWS, stride=SHARE), :] = swept(
                table_ref[k, e] & (BLOCKS - 1), table_ref[k, 32 + e] & 15, table_ref[k, 64 + e] & 15
            )
        sbuf[k, 0:HEAD] = jnp.concatenate([index_ref[k], jnp.zeros((8, 128), f32)], axis=0).astype(bf16)
        for t in range(TRACERS):
            sbuf[k, HEAD + t * PART : HEAD + (t + 1) * PART] = stage[t * PART : (t + 1) * PART, :].astype(bf16)

    def span(t):
        return pl.ds(0, HEAD + PART) if t == 0 else pl.ds(HEAD + t * PART, PART)

    def send(t, k):
        return pltpu.make_async_remote_copy(
            src_ref=sbuf.at[k, span(t)], dst_ref=rbuf.at[k, span(t)],
            send_sem=send_sem.at[t], recv_sem=recv_sem.at[t],
            device_id=(tile_of(k), lev), device_id_type=MESH,
        )

    def wait_bytes(buf, t, sem):
        ref = buf.at[pl.ds(1, TILES - 1), span(t)]
        pltpu.make_async_copy(ref, ref, sem).wait()

    def ring(j, way):
        item = x * ZN + (z - way * j + ZN) % ZN
        rows = pl.ds(0, MSG) if j < 3 else (pl.ds(0, HALF) if way > 0 else pl.ds(HALF, MSG - HALF))
        d = 0 if way > 0 else 1
        return pltpu.make_async_remote_copy(
            src_ref=sbuf.at[TILES, rows] if j == 0 else ebuf.at[item, rows],
            dst_ref=ebuf.at[item, rows],
            send_sem=ring_send.at[d, j], recv_sem=ring_recv.at[d, j],
            device_id=(tile_at(0, way), lev), device_id_type=MESH,
        )

    def cross(n):
        way = 1 if n % 2 == 0 else -1
        first = (x if n < 2 else (x - way + XN) % XN) * ZN
        group = pl.ds(first, ZN) if n < 2 else pl.ds(first if way > 0 else first + ZN // 2, ZN // 2)
        return pltpu.make_async_remote_copy(
            src_ref=ebuf.at[group], dst_ref=ebuf.at[group],
            send_sem=cross_send.at[n], recv_sem=cross_recv.at[n],
            device_id=(tile_at(way, 0), lev), device_id_type=MESH,
        )

    def keep(src, dst, i):
        return pltpu.make_async_copy(src, dst, local_sem.at[i])

    keep_extra = keep(sbuf.at[TILES], ebuf.at[me], 0)
    keep_main = keep(sbuf.at[0], rbuf.at[0], 1)
    stops = STOPS

    def step(i, carry):
        p = i - 1
        side = jnp.where(p % 2 == 0, p // 8 + 1, ZN - 1 - p // 8)
        dz = jnp.where(p < 24, side, jnp.where(p < 28, ZN // 2, 0))
        dx = jnp.where(p < 24, (p % 8) // 2, jnp.where(p < 28, p - 24, p - 27))
        k = jnp.where(i == 0, TILES, jnp.where(i == TILES, 0, dx * ZN + dz))
        build(k)

        @pl.when(i == 0)
        def _():
            pl.semaphore_wait(barrier, TILES + 1)
            ring(0, 1).start()
            ring(0, -1).start()
            keep_extra.start()

        @pl.when(jnp.logical_and(i > 0, i < TILES))
        def _():
            send(0, k).start()

        for j, stop in enumerate(stops):
            @pl.when(i == stop)
            def _():
                for way in (1, -1):
                    ring(j, way).wait_recv()
                if j < 3:
                    for way in (1, -1):
                        ring(j + 1, way).start()
                else:
                    keep_extra.wait()

        return carry

    lax.fori_loop(0, TILES + 1, step, 0)
    keep_main.start()

    def send_phase(t):
        def one(k, carry):
            send(t, k).start()
            return carry

        lax.fori_loop(1, TILES, one, 0)

    send_phase(1)
    cross(0).start()
    cross(1).start()

    def own_step(g, carry):
        for u in range(8):
            b = g * 8 + u
            own[pl.ds(b, ROWS, stride=PITCH), :] = swept(b, self_ref[0, b] & 15, self_ref[1, b] & 15)
        return carry

    lax.fori_loop(0, BLOCKS // 8, own_step, 0)
    wait_bytes(sbuf, 0, send_sem.at[0])
    send_phase(2)

    tap_row = lax.broadcasted_iota(i32, (TAP * LEVS, BLOCKS), 0)
    source = lev * LEVS + tap_row % LEVS + tap_row // LEVS - REACH
    plain = vertical_ref[...] + jnp.where(tap_row // LEVS == REACH, 1.0, 0.0)
    turned[:, : TAP * LEVS] = jnp.where(jnp.logical_and(source >= 0, source < LEVS * LEVS), plain, 0.0).T

    def spread(g, carry):
        rows = pl.ds(pl.multiple_of(g * 8, 8), 8)
        columns = turned[rows, :]
        for n in range(TAP * LEVS):
            weight[n, rows] = jnp.broadcast_to(columns[:, n : n + 1], (8, CELLS))
        return carry

    lax.fori_loop(0, BLOCKS // 8, spread, 0)
    for n in range(2):
        cross(n).wait_recv()
    for n in range(2, 4):
        cross(n).start()
    wait_bytes(sbuf, 1, send_sem.at[1])
    send_phase(3)

    def choose(buf, first, hot):
        def add(s, tile):
            return tile + buf[s, 0:HEAD].astype(f32)

        tile = lax.fori_loop(0, TILES, add, jnp.zeros((HEAD, 128), f32))
        block = lax.broadcasted_iota(i32, (BLOCKS, 128), 0).astype(f32) + 1.0
        for m in range(SLOTS // 128):
            row = tile[m : m + 1]
            if hot is not None:
                row = row * hot
            hit = (jnp.broadcast_to(row, (BLOCKS, 128)) == block).astype(f32)
            chosen[:, first + 128 * m : first + 128 * (m + 1)] = hit.astype(bf16)

    def halo(t, way):
        inner = pl.ds(LEVS, REACH) if way > 0 else pl.ds(REACH, REACH)
        outer = pl.ds(0, REACH) if way > 0 else pl.ds(LEVS + REACH, REACH)
        d = 0 if way > 0 else 1
        return pltpu.make_async_remote_copy(
            src_ref=pad.at[t, inner], dst_ref=pad.at[t, outer],
            send_sem=halo_send.at[d, t], recv_sem=halo_recv.at[d, t],
            device_id=(me, above if way > 0 else below), device_id_type=MESH,
        )

    def gather_sum(t):
        def pair(q, carry):
            rows = pl.ds(pl.multiple_of(HEAD + t * PART + q * 2 * SHARE, 16), 2 * SHARE)
            pieces = [buf[s, rows].astype(f32) for buf in (rbuf, ebuf) for s in range(TILES)]
            even = jnp.concatenate([p[:SHARE] for p in pieces], axis=0).astype(bf16)
            odd = jnp.concatenate([p[SHARE:] for p in pieces], axis=0).astype(bf16)
            both = dot(chosen[...], jnp.concatenate([even, odd], axis=1))
            for h in range(2):
                r = t * LEVS + 2 * q + h
                mine = own[pl.ds(pl.multiple_of(r * PITCH, 8), BLOCKS), :]
                pad[t, REACH + 2 * q + h] = (mine + both[:, h * CELLS : (h + 1) * CELLS]).astype(bf16)
            for n, way in ((1, -1), (3, 1)):
                @pl.when(q == n)
                def _():
                    halo(t, way).start()

            return carry

        lax.fori_loop(0, LEVS // 2, pair, 0)

    def write_out(t):
        return pltpu.make_async_copy(obuf.at[:, t], out_ref.at[:, t], out_sem.at[t])

    def remap(t):
        def chunk(g, carry):
            rows = pl.ds(pl.multiple_of(g * 16, 16), 16)
            levels = [pad[t, m, rows].astype(f32) for m in range(LEVS + 2 * REACH)]
            for l in range(LEVS):
                total = weight[l, rows] * levels[l]
                for n in range(1, TAP):
                    total = total + weight[n * LEVS + l, rows] * levels[l + n]
                turn[pl.ds(l, 16, stride=LEVS), :] = total
            for b in range(16):
                obuf[g * 16 + b, t] = turn[b * LEVS : (b + 1) * LEVS, :].astype(bf16)
            return carry

        lax.fori_loop(0, BLOCKS // 16, chunk, 0)
        write_out(t).start()

    def finish(t):
        for way in (1, -1):
            halo(t, way).wait_recv()
        remap(t)

    keep_main.wait()
    for t in range(TRACERS):
        wait_bytes(rbuf, t, recv_sem.at[t])
        if t == 0:
            for n in range(2, 4):
                cross(n).wait_recv()
            choose(rbuf, 0, None)
            choose(ebuf, SLOTS, index_ref[39][0:1])
        gather_sum(t)
        if t > 0:
            finish(t - 1)
    finish(TRACERS - 1)
    for t in range(TRACERS):
        write_out(t).wait()
        if t > 1:
            wait_bytes(sbuf, t, send_sem.at[t])
        for way in (1, -1):
            halo(t, way).wait_send()
    for n in range(4):
        for way in (1, -1):
            ring(n, way).wait_send()
        cross(n).wait_send()


def on_device(tracers, sweeps, targets, matrix_ids, self_ids, vertical):
    vmem = pl.BlockSpec(memory_space=pltpu.VMEM)
    smem = pl.BlockSpec(memory_space=pltpu.SMEM)
    hbm = pl.BlockSpec(memory_space=pl.ANY)
    dma = pltpu.SemaphoreType.DMA
    return pl.pallas_call(
        main_kernel,
        name="remap",
        out_shape=jax.ShapeDtypeStruct((BLOCKS, TRACERS, LEVS, CELLS), bf16),
        in_specs=[vmem, vmem, smem, hbm, hbm, hbm],
        out_specs=hbm,
        scratch_shapes=[
            pltpu.VMEM((BLOCKS, ROWS, CELLS), bf16),
            pltpu.VMEM((32, CELLS, CELLS), bf16),
            pltpu.VMEM((TAP * LEVS, BLOCKS), f32),
            pltpu.VMEM((40, 128), i32),
            pltpu.SMEM((40, 128), i32),
            pltpu.VMEM((40, 8, 128), f32),
            pltpu.VMEM((SHARE * ROWS, CELLS), f32),
            pltpu.VMEM((TILES + 1, MSG, CELLS), bf16),
            pltpu.VMEM((TILES, MSG, CELLS), bf16),
            pltpu.VMEM((TILES, MSG, CELLS), bf16),
            pltpu.VMEM((ROWS * PITCH, CELLS), f32),
            pltpu.VMEM((BLOCKS, 2 * SLOTS), bf16),
            pltpu.VMEM((TRACERS, LEVS + 2 * REACH, BLOCKS, CELLS), bf16),
            pltpu.VMEM((BLOCKS, 128), f32),
            pltpu.VMEM((TAP * LEVS, BLOCKS, CELLS), f32),
            pltpu.VMEM((16 * LEVS, CELLS), f32),
            pltpu.VMEM((BLOCKS, TRACERS, LEVS, CELLS), bf16),
            dma((4,)), dma((TRACERS,)), dma((TRACERS,)), dma((2, 4)), dma((2, 4)), dma((4,)), dma((4,)),
            dma((2, TRACERS)), dma((2, TRACERS)), dma((2,)), dma((TRACERS,)),
        ],
        compiler_params=pltpu.CompilerParams(
            collective_id=0, has_side_effects=True, vmem_limit_bytes=56 * 1024 * 1024
        ),
    )(
        targets.T,
        jnp.transpose(matrix_ids, (1, 2, 0)),
        self_ids.T,
        tracers.reshape(BLOCKS, ROWS, CELLS),
        sweeps.reshape(-1, CELLS, CELLS),
        vertical.reshape(TAP * LEVS, BLOCKS),
    )


def solution(mesh):
    placed = (
        P("tile", None, "lev", None),
        P(),
        P("tile", None),
        P("tile", None, None),
        P("tile", None),
        P(None, "lev", "tile"),
    )
    return jax.shard_map(
        on_device,
        mesh=mesh,
        in_specs=placed,
        out_specs=P("tile", None, "lev", None),
        check_vma=False,
    )
```

time: 220 us -> 179 us (0.81); the launches traced: 216 us -> 178 us
  Pallas kernels: 208 us -> 175 us
  local copies, waits for them, and re-layouts: 5.73 us -> 3.27 us
    pallas_call x1, Pallas kernels: 205 us -> 175 us  [on_device(): pl.pallas_call(main_kernel, name='remap', out_shape=jax.ShapeDtypeStruct(...]
    reshape x2 -> x0, local copies, waits for them, and re-layouts: 4.96 us -> none  [the longest x1 4.26 us: on_device(): return jnp.transpose(out, (1, 0, 2)).reshape(BLOCKS, TRACERS, LEVS, CELLS)]
    pallas_call x1 -> x0, Pallas kernels: 3.44 us -> none  [on_device(): pl.pallas_call(plan_kernel, name='plan', out_shape=(jax.ShapeDtypeStruct(...]
    unnamed x0 -> x1, local copies, waits for them, and re-layouts: none -> 3.27 us
where the time goes in v2:
time: 179 us; the launch traced here: 178 us
  Pallas kernels  175 us (98%)
  local copies, waits for them, and re-layouts  3.27 us (2%)
    pallas_call x1, Pallas kernels, on_device(): pl.pallas_call(main_kernel, name='remap', out_shape=jax.ShapeDtypeStruct(...  175 us

profile of v2, /device:TPU:1, one launch (start us, length us, event | category | flops | bytes accessed | tf_op | source)
XLA Modules:
  0.0 178.4 jit_solution(185414015461755822)
XLA Ops:
  0.0 175.2 %remap.1 = bf16[256,4,8,128]{3,2,1,0:T(8,128)(2,1)} custom-call(s32[3,256]{1,0:T(4,128)} %bitcast.10, s32[3,2,256]{2,1,0:T(2,128)} %bitcast.9, s32[2,256]{1,0:T(2,128)} %bitcast.11, bf16[256,32,128]{2,1,0:T(8,128)(2,1)} %bitcast.6, bf16[32,128,128]{2,1,0:T(8,128)(2,1)} %bitcast.7, f32[72,256]{1,0:T(8,128)} %bitcast.8), custom_call_target="tpu_custom_call" | custom-call | tf_op jit(solution)/shard_map/remap/pallas_call | solution.py:342
  175.2 3.3 %copy.8 = bf16[256,4,8,128]{3,2,1,0:T(8,128)(2,1)} copy(bf16[256,4,8,128]{3,2,1,0:T(8,128)(2,1)} %remap.1) | data formatting | bytes 4194304

commit v3 on v2

--- a/solution.py
+++ b/solution.py
@@ -24,8 +24,13 @@
 HALF = 384
 PITCH = BLOCKS + 8
 SLOTS = TILES * SHARE
-STOPS = (5, 10, 15, 20)
+STOPS = (4, 8, 12, 16)
+PHASES = TRACERS + 1
 f32, bf16, i32 = jnp.float32, jnp.bfloat16, jnp.int32
+
+
+def ORDER(i):
+    return jnp.where(i % 2 == 0, TILES - 2 - i // 2, i // 2)
 
 
 def dot(a, b):
@@ -34,7 +39,7 @@
 
 def main_kernel(
     target_ref, matrix_ref, self_ref, tracers_in, sweeps_in, vertical_in, out_ref,
-    tracers_ref, sweeps_ref, vertical_ref, table_made, table_ref, index_ref,
+    tracers_ref, sweeps_ref, vertical_ref, table_made, table_ref, head, hot,
     stage, sbuf, rbuf, ebuf, own, chosen, pad, turned, weight, turn, obuf,
     in_sem, send_sem, recv_sem, ring_send, ring_recv, cross_send, cross_recv, halo_send, halo_recv, local_sem, out_sem,
 ):
@@ -68,6 +73,9 @@
         pl.semaphore_signal(barrier, inc=1, device_id=(me, other), device_id_type=MESH)
 
     def plan():
+        def over_blocks(a, b):
+            return lax.dot_general(a, b.astype(bf16), (((1,), (1,)), ((), ())), preferred_element_type=f32)
+
         sub = lax.broadcasted_iota(i32, (40, BLOCKS), 0)
         slot = lax.broadcasted_iota(i32, (SLOTS, BLOCKS), 0)
         block = lax.broadcasted_iota(i32, (1, BLOCKS), 1).astype(f32)
@@ -75,7 +83,8 @@
             lax.broadcasted_iota(i32, (BLOCKS, BLOCKS), 0) < lax.broadcasted_iota(i32, (BLOCKS, BLOCKS), 1)
         ).astype(f32).astype(bf16)
         base = jnp.zeros((40, 1), f32)
-        total = None
+        line = lax.broadcasted_iota(i32, (8, BLOCKS), 0)
+        total, index = None, None
         for j in range(3):
             target = target_ref[j : j + 1, :]
             owner = target >> 8
@@ -93,17 +102,19 @@
             arrival = ((target & (BLOCKS - 1)) + 1).astype(f32)
             ids = matrix_ref[j].astype(f32)
             at = (jnp.broadcast_to(order, (SLOTS, BLOCKS)) == slot).astype(f32)
-            values = jnp.concatenate(
-                [at_entry * block, at_entry * ids[0:1], at_entry * ids[1:2], at_entry, at * arrival], axis=0
-            ).astype(bf16)
-            part = lax.dot_general(taken, values, (((1,), (1,)), ((), ())), preferred_element_type=f32)
+            values = jnp.concatenate([at_entry * block, at_entry * ids[0:1], at_entry * ids[1:2], at_entry], axis=0)
+            part = over_blocks(taken, values)
             total = part if total is None else total + part
-        table_made[...] = total[:, :128].astype(i32)
+            kind = (jnp.broadcast_to(extra.astype(i32), (8, BLOCKS)) == line).astype(f32).astype(bf16)
+            part = over_blocks(kind, at * arrival)
+            index = part if index is None else index + part
+        table_made[...] = total.astype(i32)
+        head[...] = jnp.zeros((HEAD, 128), f32)
         for m in range(SLOTS // 128):
-            index_ref[:, m, :] = total[:, 128 * (m + 1) : 128 * (m + 2)]
-        for m in range(SLOTS // 128, 8):
-            index_ref[:, m, :] = jnp.zeros((40, 128), f32)
-        index_ref[39] = jnp.broadcast_to((base[0:1] > SHARE).astype(f32), (8, 128))
+            head[m : m + 1] = index[0:1, 128 * m : 128 * (m + 1)]
+            head[8 + m : 9 + m] = index[1:2, 128 * m : 128 * (m + 1)]
+        sbuf[TILES, 0:HEAD] = head[...].astype(bf16)
+        hot[...] = jnp.broadcast_to((base[0:1] > SHARE).astype(f32), (8, 128))
         copy = pltpu.make_async_copy(table_made, table_ref, in_sem.at[3])
         copy.start()
         copy.wait()
@@ -121,12 +132,19 @@
             stage[pl.ds(e, ROWS, stride=SHARE), :] = swept(
                 table_ref[k, e] & (BLOCKS - 1), table_ref[k, 32 + e] & 15, table_ref[k, 64 + e] & 15
             )
-        sbuf[k, 0:HEAD] = jnp.concatenate([index_ref[k], jnp.zeros((8, 128), f32)], axis=0).astype(bf16)
         for t in range(TRACERS):
             sbuf[k, HEAD + t * PART : HEAD + (t + 1) * PART] = stage[t * PART : (t + 1) * PART, :].astype(bf16)
 
-    def span(t):
-        return pl.ds(0, HEAD + PART) if t == 0 else pl.ds(HEAD + t * PART, PART)
+    first_half = lev % 2
+
+    def half_of(s):
+        return first_half if s == TRACERS - 1 else 1 - first_half
+
+    def span(s):
+        if s < TRACERS - 1 or PHASES == TRACERS:
+            return pl.ds(HEAD + s * PART, PART)
+        start = HEAD + (TRACERS - 1) * PART + half_of(s) * (PART // 2)
+        return pl.ds(pl.multiple_of(start, 16), PART // 2)
 
     def send(t, k):
         return pltpu.make_async_remote_copy(
@@ -165,14 +183,16 @@
 
     keep_extra = keep(sbuf.at[TILES], ebuf.at[me], 0)
     keep_main = keep(sbuf.at[0], rbuf.at[0], 1)
-    stops = STOPS
-
-    def step(i, carry):
-        p = i - 1
+    def partner(p):
         side = jnp.where(p % 2 == 0, p // 8 + 1, ZN - 1 - p // 8)
         dz = jnp.where(p < 24, side, jnp.where(p < 28, ZN // 2, 0))
         dx = jnp.where(p < 24, (p % 8) // 2, jnp.where(p < 28, p - 24, p - 27))
-        k = jnp.where(i == 0, TILES, jnp.where(i == TILES, 0, dx * ZN + dz))
+        return dx * ZN + dz
+
+    stops = STOPS
+
+    def step(i, carry):
+        k = jnp.where(i == 0, TILES, jnp.where(i == TILES, 0, partner(i - 1)))
         build(k)
 
         @pl.when(i == 0)
@@ -203,11 +223,11 @@
     keep_main.start()
 
     def send_phase(t):
-        def one(k, carry):
-            send(t, k).start()
+        def one(i, carry):
+            send(t, partner(ORDER(i))).start()
             return carry
 
-        lax.fori_loop(1, TILES, one, 0)
+        lax.fori_loop(0, TILES - 1, one, 0)
 
     send_phase(1)
     cross(0).start()
@@ -242,32 +262,37 @@
         cross(n).start()
     wait_bytes(sbuf, 1, send_sem.at[1])
     send_phase(3)
-
-    def choose(buf, first, hot):
-        def add(s, tile):
-            return tile + buf[s, 0:HEAD].astype(f32)
-
-        tile = lax.fori_loop(0, TILES, add, jnp.zeros((HEAD, 128), f32))
+    send_phase(4)
+
+    def choose():
+        lane = lax.broadcasted_iota(i32, (8, 128), 0) * 128 + lax.broadcasted_iota(i32, (8, 128), 1)
+
+        def add(s, sums):
+            tile = ebuf[s, 0:HEAD].astype(f32)
+            k = ((x - s // ZN + XN) % XN) * ZN + (z - s % ZN + ZN) % ZN
+            mine = jnp.logical_and(lane >= k * SHARE, lane < (k + 1) * SHARE)
+            return sums[0] + jnp.where(mine, tile[0:8], 0.0), sums[1] + tile[8:16]
+
+        none = jnp.zeros((8, 128), f32)
+        main, extra = lax.fori_loop(0, TILES, add, (none, none))
+        extra = extra * hot[...]
         block = lax.broadcasted_iota(i32, (BLOCKS, 128), 0).astype(f32) + 1.0
-        for m in range(SLOTS // 128):
-            row = tile[m : m + 1]
-            if hot is not None:
-                row = row * hot
-            hit = (jnp.broadcast_to(row, (BLOCKS, 128)) == block).astype(f32)
-            chosen[:, first + 128 * m : first + 128 * (m + 1)] = hit.astype(bf16)
-
-    def halo(t, way):
-        inner = pl.ds(LEVS, REACH) if way > 0 else pl.ds(REACH, REACH)
-        outer = pl.ds(0, REACH) if way > 0 else pl.ds(LEVS + REACH, REACH)
-        d = 0 if way > 0 else 1
+        for first, tile in ((0, main), (SLOTS, extra)):
+            for m in range(SLOTS // 128):
+                hit = (jnp.broadcast_to(tile[m : m + 1], (BLOCKS, 128)) == block).astype(f32)
+                chosen[:, first + 128 * m : first + 128 * (m + 1)] = hit.astype(bf16)
+
+    def halo(t, half):
         return pltpu.make_async_remote_copy(
-            src_ref=pad.at[t, inner], dst_ref=pad.at[t, outer],
-            send_sem=halo_send.at[d, t], recv_sem=halo_recv.at[d, t],
-            device_id=(me, above if way > 0 else below), device_id_type=MESH,
+            src_ref=pad.at[t, pl.ds(REACH + REACH * half, REACH)],
+            dst_ref=pad.at[t, pl.ds((LEVS + REACH) * (1 - half), REACH)],
+            send_sem=halo_send.at[half, t], recv_sem=halo_recv.at[half, t],
+            device_id=(me, (lev + LEVS - 1 + 2 * half) % LEVS), device_id_type=MESH,
         )
 
-    def gather_sum(t):
-        def pair(q, carry):
+    def gather_sum(t, half):
+        def pair(n, carry):
+            q = half * 2 + n
             rows = pl.ds(pl.multiple_of(HEAD + t * PART + q * 2 * SHARE, 16), 2 * SHARE)
             pieces = [buf[s, rows].astype(f32) for buf in (rbuf, ebuf) for s in range(TILES)]
             even = jnp.concatenate([p[:SHARE] for p in pieces], axis=0).astype(bf16)
@@ -277,17 +302,14 @@
                 r = t * LEVS + 2 * q + h
                 mine = own[pl.ds(pl.multiple_of(r * PITCH, 8), BLOCKS), :]
                 pad[t, REACH + 2 * q + h] = (mine + both[:, h * CELLS : (h + 1) * CELLS]).astype(bf16)
-            for n, way in ((1, -1), (3, 1)):
-                @pl.when(q == n)
-                def _():
-                    halo(t, way).start()
-
             return carry
 
-        lax.fori_loop(0, LEVS // 2, pair, 0)
-
-    def write_out(t):
-        return pltpu.make_async_copy(obuf.at[:, t], out_ref.at[:, t], out_sem.at[t])
+        lax.fori_loop(0, 2, pair, 0)
+        halo(t, half).start()
+
+    def write_out(t, c):
+        part = pl.ds(c * (BLOCKS // 4), BLOCKS // 4)
+        return pltpu.make_async_copy(obuf.at[part, t], out_ref.at[part, t], out_sem.at[t, c])
 
     def remap(t):
         def chunk(g, carry):
@@ -300,38 +322,59 @@
                 turn[pl.ds(l, 16, stride=LEVS), :] = total
             for b in range(16):
                 obuf[g * 16 + b, t] = turn[b * LEVS : (b + 1) * LEVS, :].astype(bf16)
+
+            @pl.when(g % 4 == 3)
+            def _():
+                write_out(t, g // 4).start()
+
             return carry
 
         lax.fori_loop(0, BLOCKS // 16, chunk, 0)
-        write_out(t).start()
 
     def finish(t):
-        for way in (1, -1):
-            halo(t, way).wait_recv()
+        for half in range(2):
+            halo(t, half).wait_recv()
         remap(t)
 
     keep_main.wait()
-    for t in range(TRACERS):
-        wait_bytes(rbuf, t, recv_sem.at[t])
-        if t == 0:
+    for s in range(PHASES):
+        wait_bytes(rbuf, s, recv_sem.at[s])
+        if s == 0:
             for n in range(2, 4):
                 cross(n).wait_recv()
-            choose(rbuf, 0, None)
-            choose(ebuf, SLOTS, index_ref[39][0:1])
-        gather_sum(t)
-        if t > 0:
-            finish(t - 1)
+            choose()
+        if s < TRACERS - 1 or PHASES == TRACERS:
+            gather_sum(s, first_half)
+            gather_sum(s, 1 - first_half)
+        else:
+            gather_sum(TRACERS - 1, half_of(s))
+        if 0 < s < TRACERS:
+            finish(s - 1)
     finish(TRACERS - 1)
+    for s in range(2, PHASES):
+        wait_bytes(sbuf, s, send_sem.at[s])
     for t in range(TRACERS):
-        write_out(t).wait()
-        if t > 1:
-            wait_bytes(sbuf, t, send_sem.at[t])
-        for way in (1, -1):
-            halo(t, way).wait_send()
+        for c in range(4):
+            write_out(t, c).wait()
+        for half in range(2):
+            halo(t, half).wait_send()
     for n in range(4):
         for way in (1, -1):
             ring(n, way).wait_send()
         cross(n).wait_send()
+
+
+def hand_on(given_ref, out_ref, held, in_sem, out_sem):
+    parts = [pl.ds(n * (BLOCKS // 4), BLOCKS // 4) for n in range(4)]
+    loads = [pltpu.make_async_copy(given_ref.at[p], held.at[p], in_sem.at[n]) for n, p in enumerate(parts)]
+    stores = [pltpu.make_async_copy(held.at[p], out_ref.at[p], out_sem.at[n]) for n, p in enumerate(parts)]
+    for load in loads:
+        load.start()
+    for load, store in zip(loads, stores):
+        load.wait()
+        store.start()
+    for store in stores:
+        store.wait()
 
 
 def on_device(tracers, sweeps, targets, matrix_ids, self_ids, vertical):
@@ -339,7 +382,7 @@
     smem = pl.BlockSpec(memory_space=pltpu.SMEM)
     hbm = pl.BlockSpec(memory_space=pl.ANY)
     dma = pltpu.SemaphoreType.DMA
-    return pl.pallas_call(
+    remapped = pl.pallas_call(
         main_kernel,
         name="remap",
         out_shape=jax.ShapeDtypeStruct((BLOCKS, TRACERS, LEVS, CELLS), bf16),
@@ -351,7 +394,8 @@
             pltpu.VMEM((TAP * LEVS, BLOCKS), f32),
             pltpu.VMEM((40, 128), i32),
             pltpu.SMEM((40, 128), i32),
-            pltpu.VMEM((40, 8, 128), f32),
+            pltpu.VMEM((HEAD, 128), f32),
+            pltpu.VMEM((8, 128), f32),
             pltpu.VMEM((SHARE * ROWS, CELLS), f32),
             pltpu.VMEM((TILES + 1, MSG, CELLS), bf16),
             pltpu.VMEM((TILES, MSG, CELLS), bf16),
@@ -363,8 +407,8 @@
             pltpu.VMEM((TAP * LEVS, BLOCKS, CELLS), f32),
             pltpu.VMEM((16 * LEVS, CELLS), f32),
             pltpu.VMEM((BLOCKS, TRACERS, LEVS, CELLS), bf16),
-            dma((4,)), dma((TRACERS,)), dma((TRACERS,)), dma((2, 4)), dma((2, 4)), dma((4,)), dma((4,)),
-            dma((2, TRACERS)), dma((2, TRACERS)), dma((2,)), dma((TRACERS,)),
+            dma((4,)), dma((PHASES,)), dma((PHASES,)), dma((2, 4)), dma((2, 4)), dma((4,)), dma((4,)),
+            dma((2, TRACERS)), dma((2, TRACERS)), dma((2,)), dma((TRACERS, 4)),
         ],
         compiler_params=pltpu.CompilerParams(
             collective_id=0, has_side_effects=True, vmem_limit_bytes=56 * 1024 * 1024
@@ -377,6 +421,15 @@
         sweeps.reshape(-1, CELLS, CELLS),
         vertical.reshape(TAP * LEVS, BLOCKS),
     )
+    return pl.pallas_call(
+        hand_on,
+        name="hand_on",
+        out_shape=jax.ShapeDtypeStruct(remapped.shape, bf16),
+        in_specs=[hbm],
+        out_specs=hbm,
+        scratch_shapes=[pltpu.VMEM(remapped.shape, bf16), dma((4,)), dma((4,))],
+        compiler_params=pltpu.CompilerParams(vmem_limit_bytes=56 * 1024 * 1024),
+    )(remapped)
 
 
 def solution(mesh):

time: 179 us -> 172 us (0.961)
  local copies, waits for them, and re-layouts: 3.27 us -> 0 us
  Pallas kernels: 175 us -> 172 us
    pallas_call x1, Pallas kernels: 175 us -> 169 us  [on_device(): pl.pallas_call(main_kernel, name='remap', out_shape=jax.ShapeDtypeStruct(...]
    unnamed x1 -> x0, local copies, waits for them, and re-layouts: 3.27 us -> none
    pallas_call x0 -> x1, Pallas kernels: none -> 2.42 us  [on_device(): pl.pallas_call(hand_on, name='hand_on', out_shape=jax.ShapeDtypeStruct(re...]
where the time goes in v3:
time: 172 us
  Pallas kernels  172 us (100%)
    pallas_call x1, Pallas kernels, on_device(): pl.pallas_call(main_kernel, name='remap', out_shape=jax.ShapeDtypeStruct(...  169 us

profile of v3, /device:TPU:1, one launch (start us, length us, event | category | flops | bytes accessed | tf_op | source)
XLA Modules:
  0.0 171.8 jit_solution(9882272999860335017)
XLA Ops:
  0.0 169.3 %remap.1.given_ref = bf16[256,4,8,128]{3,2,1,0:T(8,128)(2,1)} custom-call(s32[3,256]{1,0:T(4,128)} %bitcast.10, s32[3,2,256]{2,1,0:T(2,128)} %bitcast.9, s32[2,256]{1,0:T(2,128)} %bitcast.11, bf16[256,32,128]{2,1,0:T(8,128)(2,1)} %bitcast.6, bf16[32,128,128]{2,1,0:T(8,128)(2,1)} %bitcast.7, f32[72,256]{1,0:T(8,128)} %bitcast.8), custom_call_target="tpu_custom_call" | custom-call | tf_op jit(solution)/shard_map/remap/pallas_call | solution.py:385
  169.3 2.4 %hand_on.1 = bf16[256,4,8,128]{3,2,1,0:T(8,128)(2,1)} custom-call(bf16[256,4,8,128]{3,2,1,0:T(8,128)(2,1)} %remap.1.given_ref), custom_call_target="tpu_custom_call" | custom-call | tf_op jit(solution)/shard_map/hand_on/pallas_call | solution.py:424

commit v4 on v3

--- a/solution.py
+++ b/solution.py
@@ -40,15 +40,18 @@
 def main_kernel(
     target_ref, matrix_ref, self_ref, tracers_in, sweeps_in, vertical_in, out_ref,
     tracers_ref, sweeps_ref, vertical_ref, table_made, table_ref, head, hot,
-    stage, sbuf, rbuf, ebuf, own, chosen, pad, turned, weight, turn, obuf,
-    in_sem, send_sem, recv_sem, ring_send, ring_recv, cross_send, cross_recv, halo_send, halo_recv, local_sem, out_sem,
+    stage, sbuf, rbuf, ebuf, own, chosen, pad, turned, weight, turn,
+    in_sem, send_sem, recv_sem, ring_send, ring_recv, cross_send, cross_recv, halo_send, halo_recv, local_sem,
 ):
     me = lax.axis_index("tile")
     lev = lax.axis_index("lev")
     x, z = me // ZN, me % ZN
 
+    def wrap(v, n):
+        return jnp.where(v >= n, v - n, v)
+
     def tile_at(dx, dz):
-        return ((x + dx + XN) % XN) * ZN + (z + dz + ZN) % ZN
+        return wrap(x + dx, XN) * ZN + wrap(z + dz, ZN)
 
     def tile_of(k):
         return tile_at(k // ZN, k % ZN)
@@ -63,11 +66,10 @@
         load.start()
     barrier = pltpu.get_barrier_semaphore()
 
-    def greet(k, carry):
-        pl.semaphore_signal(barrier, inc=1, device_id=(tile_of(k), lev), device_id_type=MESH)
-        return carry
-
-    lax.fori_loop(1, TILES, greet, 0)
+    for dx in range(XN):
+        for dz in range(ZN):
+            if dx or dz:
+                pl.semaphore_signal(barrier, inc=1, device_id=(tile_at(dx, dz), lev), device_id_type=MESH)
     above, below = (lev + 1) % LEVS, (lev + LEVS - 1) % LEVS
     for other in (above, below):
         pl.semaphore_signal(barrier, inc=1, device_id=(me, other), device_id_type=MESH)
@@ -165,7 +167,7 @@
             src_ref=sbuf.at[TILES, rows] if j == 0 else ebuf.at[item, rows],
             dst_ref=ebuf.at[item, rows],
             send_sem=ring_send.at[d, j], recv_sem=ring_recv.at[d, j],
-            device_id=(tile_at(0, way), lev), device_id_type=MESH,
+            device_id=(tile_at(0, way % ZN), lev), device_id_type=MESH,
         )
 
     def cross(n):
@@ -175,7 +177,7 @@
         return pltpu.make_async_remote_copy(
             src_ref=ebuf.at[group], dst_ref=ebuf.at[group],
             send_sem=cross_send.at[n], recv_sem=cross_recv.at[n],
-            device_id=(tile_at(way, 0), lev), device_id_type=MESH,
+            device_id=(tile_at(way % XN, 0), lev), device_id_type=MESH,
         )
 
     def keep(src, dst, i):
@@ -307,10 +309,6 @@
         lax.fori_loop(0, 2, pair, 0)
         halo(t, half).start()
 
-    def write_out(t, c):
-        part = pl.ds(c * (BLOCKS // 4), BLOCKS // 4)
-        return pltpu.make_async_copy(obuf.at[part, t], out_ref.at[part, t], out_sem.at[t, c])
-
     def remap(t):
         def chunk(g, carry):
             rows = pl.ds(pl.multiple_of(g * 16, 16), 16)
@@ -321,12 +319,7 @@
                     total = total + weight[n * LEVS + l, rows] * levels[l + n]
                 turn[pl.ds(l, 16, stride=LEVS), :] = total
             for b in range(16):
-                obuf[g * 16 + b, t] = turn[b * LEVS : (b + 1) * LEVS, :].astype(bf16)
-
-            @pl.when(g % 4 == 3)
-            def _():
-                write_out(t, g // 4).start()
-
+                out_ref[g * 16 + b, t] = turn[b * LEVS : (b + 1) * LEVS, :].astype(bf16)
             return carry
 
         lax.fori_loop(0, BLOCKS // 16, chunk, 0)
@@ -354,8 +347,6 @@
     for s in range(2, PHASES):
         wait_bytes(sbuf, s, send_sem.at[s])
     for t in range(TRACERS):
-        for c in range(4):
-            write_out(t, c).wait()
         for half in range(2):
             halo(t, half).wait_send()
     for n in range(4):
@@ -364,30 +355,17 @@
         cross(n).wait_send()
 
 
-def hand_on(given_ref, out_ref, held, in_sem, out_sem):
-    parts = [pl.ds(n * (BLOCKS // 4), BLOCKS // 4) for n in range(4)]
-    loads = [pltpu.make_async_copy(given_ref.at[p], held.at[p], in_sem.at[n]) for n, p in enumerate(parts)]
-    stores = [pltpu.make_async_copy(held.at[p], out_ref.at[p], out_sem.at[n]) for n, p in enumerate(parts)]
-    for load in loads:
-        load.start()
-    for load, store in zip(loads, stores):
-        load.wait()
-        store.start()
-    for store in stores:
-        store.wait()
-
-
 def on_device(tracers, sweeps, targets, matrix_ids, self_ids, vertical):
     vmem = pl.BlockSpec(memory_space=pltpu.VMEM)
     smem = pl.BlockSpec(memory_space=pltpu.SMEM)
     hbm = pl.BlockSpec(memory_space=pl.ANY)
     dma = pltpu.SemaphoreType.DMA
-    remapped = pl.pallas_call(
+    return pl.pallas_call(
         main_kernel,
         name="remap",
-        out_shape=jax.ShapeDtypeStruct((BLOCKS, TRACERS, LEVS, CELLS), bf16),
+        out_shape=pltpu.VMEM((BLOCKS, TRACERS, LEVS, CELLS), bf16),
         in_specs=[vmem, vmem, smem, hbm, hbm, hbm],
-        out_specs=hbm,
+        out_specs=vmem,
         scratch_shapes=[
             pltpu.VMEM((BLOCKS, ROWS, CELLS), bf16),
             pltpu.VMEM((32, CELLS, CELLS), bf16),
@@ -406,9 +384,8 @@
             pltpu.VMEM((BLOCKS, 128), f32),
             pltpu.VMEM((TAP * LEVS, BLOCKS, CELLS), f32),
             pltpu.VMEM((16 * LEVS, CELLS), f32),
-            pltpu.VMEM((BLOCKS, TRACERS, LEVS, CELLS), bf16),
             dma((4,)), dma((PHASES,)), dma((PHASES,)), dma((2, 4)), dma((2, 4)), dma((4,)), dma((4,)),
-            dma((2, TRACERS)), dma((2, TRACERS)), dma((2,)), dma((TRACERS, 4)),
+            dma((2, TRACERS)), dma((2, TRACERS)), dma((2,)),
         ],
         compiler_params=pltpu.CompilerParams(
             collective_id=0, has_side_effects=True, vmem_limit_bytes=56 * 1024 * 1024
@@ -421,15 +398,6 @@
         sweeps.reshape(-1, CELLS, CELLS),
         vertical.reshape(TAP * LEVS, BLOCKS),
     )
-    return pl.pallas_call(
-        hand_on,
-        name="hand_on",
-        out_shape=jax.ShapeDtypeStruct(remapped.shape, bf16),
-        in_specs=[hbm],
-        out_specs=hbm,
-        scratch_shapes=[pltpu.VMEM(remapped.shape, bf16), dma((4,)), dma((4,))],
-        compiler_params=pltpu.CompilerParams(vmem_limit_bytes=56 * 1024 * 1024),
-    )(remapped)
 
 
 def solution(mesh):

time: 172 us -> 169 us (0.983)
  Pallas kernels: 172 us -> 168 us
    pallas_call x2 -> x1, Pallas kernels: 172 us -> 168 us  [on_device(): pl.pallas_call(main_kernel, name='remap', out_shape=pltpu.VMEM((BLOCKS, T...]
where the time goes in v4:
time: 169 us
  Pallas kernels  168 us (99%)
    pallas_call x1, Pallas kernels, on_device(): pl.pallas_call(main_kernel, name='remap', out_shape=pltpu.VMEM((BLOCKS, T...  168 us

profile of v4, /device:TPU:1, one launch (start us, length us, event | category | flops | bytes accessed | tf_op | source)
XLA Modules:
  0.0 168.8 jit_solution(17524102866752112008)
XLA Ops:
  0.0 167.5 %remap.1 = bf16[256,4,8,128]{3,2,1,0:T(8,128)(2,1)S(1)} custom-call(s32[3,256]{1,0:T(4,128)} %bitcast.10, s32[3,2,256]{2,1,0:T(2,128)} %bitcast.9, s32[2,256]{1,0:T(2,128)} %bitcast.11, bf16[256,32,128]{2,1,0:T(8,128)(2,1)} %bitcast.6, bf16[32,128,128]{2,1,0:T(8,128)(2,1)} %bitcast.7, f32[72,256]{1,0:T(8,128)} %bitcast.8), custom_call_target="tpu_custom_call" | custom-call | tf_op jit(solution)/shard_map/remap/pallas_call | solution.py:363
  167.5 1.3 copy.8

commit v5 on v4

--- a/solution.py
+++ b/solution.py
@@ -38,7 +38,8 @@
 
 
 def main_kernel(
-    target_ref, matrix_ref, self_ref, tracers_in, sweeps_in, vertical_in, out_ref,
+    target_in, matrix_in, self_in, tracers_in, sweeps_in, vertical_in, out_ref,
+    target_ref, matrix_ref, self_ref,
     tracers_ref, sweeps_ref, vertical_ref, table_made, table_ref, head, hot,
     stage, sbuf, rbuf, ebuf, own, chosen, pad, turned, weight, turn,
     in_sem, send_sem, recv_sem, ring_send, ring_recv, cross_send, cross_recv, halo_send, halo_recv, local_sem,
@@ -56,12 +57,11 @@
     def tile_of(k):
         return tile_at(k // ZN, k % ZN)
 
-    loads = [
-        pltpu.make_async_copy(src, dst, in_sem.at[n])
-        for n, (src, dst) in enumerate(
-            ((sweeps_in, sweeps_ref), (tracers_in, tracers_ref), (vertical_in, vertical_ref))
-        )
-    ]
+    moves = (
+        (target_in, target_ref), (matrix_in, matrix_ref), (self_in, self_ref),
+        (sweeps_in, sweeps_ref), (tracers_in, tracers_ref), (vertical_in, vertical_ref),
+    )
+    loads = [pltpu.make_async_copy(src, dst, in_sem.at[n]) for n, (src, dst) in enumerate(moves)]
     for load in loads:
         load.start()
     barrier = pltpu.get_barrier_semaphore()
@@ -117,12 +117,14 @@
             head[8 + m : 9 + m] = index[1:2, 128 * m : 128 * (m + 1)]
         sbuf[TILES, 0:HEAD] = head[...].astype(bf16)
         hot[...] = jnp.broadcast_to((base[0:1] > SHARE).astype(f32), (8, 128))
-        copy = pltpu.make_async_copy(table_made, table_ref, in_sem.at[3])
+        copy = pltpu.make_async_copy(table_made, table_ref, in_sem.at[6])
         copy.start()
         copy.wait()
 
+    for load in loads[:3]:
+        load.wait()
     plan()
-    for load in loads:
+    for load in loads[3:]:
         load.wait()
 
     def swept(block, first, second):
@@ -187,6 +189,7 @@
     keep_main = keep(sbuf.at[0], rbuf.at[0], 1)
     def partner(p):
         side = jnp.where(p % 2 == 0, p // 8 + 1, ZN - 1 - p // 8)
+        side = jnp.where(lev % 2 == 0, side, ZN - side)
         dz = jnp.where(p < 24, side, jnp.where(p < 28, ZN // 2, 0))
         dx = jnp.where(p < 24, (p % 8) // 2, jnp.where(p < 28, p - 24, p - 27))
         return dx * ZN + dz
@@ -284,30 +287,49 @@
                 hit = (jnp.broadcast_to(tile[m : m + 1], (BLOCKS, 128)) == block).astype(f32)
                 chosen[:, first + 128 * m : first + 128 * (m + 1)] = hit.astype(bf16)
 
-    def halo(t, half):
+    def halo(t, q):
+        half = q // 2
         return pltpu.make_async_remote_copy(
-            src_ref=pad.at[t, pl.ds(REACH + REACH * half, REACH)],
-            dst_ref=pad.at[t, pl.ds((LEVS + REACH) * (1 - half), REACH)],
-            send_sem=halo_send.at[half, t], recv_sem=halo_recv.at[half, t],
+            src_ref=pad.at[t, pl.ds(REACH + 2 * q, 2)],
+            dst_ref=pad.at[t, pl.ds(REACH + 2 * q + LEVS * (1 - 2 * half), 2)],
+            send_sem=halo_send.at[q, t], recv_sem=halo_recv.at[q, t],
             device_id=(me, (lev + LEVS - 1 + 2 * half) % LEVS), device_id_type=MESH,
         )
 
+    def slot_sums(bufs, t, q):
+        rows = pl.ds(pl.multiple_of(HEAD + t * PART + q * 2 * SHARE, 16), 2 * SHARE)
+        pieces = [buf[s, rows].astype(f32) for buf in bufs for s in range(TILES)]
+        even = jnp.concatenate([p[:SHARE] for p in pieces], axis=0).astype(bf16)
+        odd = jnp.concatenate([p[SHARE:] for p in pieces], axis=0).astype(bf16)
+        first = 0 if bufs[0] is rbuf else SLOTS
+        weights = chosen[:, first : first + SLOTS * len(bufs)]
+        return dot(weights, jnp.concatenate([even, odd], axis=1))
+
+    def own_rows(t, q, h):
+        return pl.ds(pl.multiple_of((t * LEVS + 2 * q + h) * PITCH, 8), BLOCKS)
+
+    def add_extras(t):
+        def pair(q, carry):
+            both = slot_sums((ebuf,), t, q)
+            for h in range(2):
+                own[own_rows(t, q, h), :] += both[:, h * CELLS : (h + 1) * CELLS]
+            return carry
+
+        lax.fori_loop(0, LEVS // 2, pair, 0)
+
     def gather_sum(t, half):
+        bufs = (rbuf,) if t == TRACERS - 1 else (rbuf, ebuf)
+
         def pair(n, carry):
             q = half * 2 + n
-            rows = pl.ds(pl.multiple_of(HEAD + t * PART + q * 2 * SHARE, 16), 2 * SHARE)
-            pieces = [buf[s, rows].astype(f32) for buf in (rbuf, ebuf) for s in range(TILES)]
-            even = jnp.concatenate([p[:SHARE] for p in pieces], axis=0).astype(bf16)
-            odd = jnp.concatenate([p[SHARE:] for p in pieces], axis=0).astype(bf16)
-            both = dot(chosen[...], jnp.concatenate([even, odd], axis=1))
+            both = slot_sums(bufs, t, q)
             for h in range(2):
-                r = t * LEVS + 2 * q + h
-                mine = own[pl.ds(pl.multiple_of(r * PITCH, 8), BLOCKS), :]
+                mine = own[own_rows(t, q, h), :]
                 pad[t, REACH + 2 * q + h] = (mine + both[:, h * CELLS : (h + 1) * CELLS]).astype(bf16)
+            halo(t, q).start()
             return carry
 
         lax.fori_loop(0, 2, pair, 0)
-        halo(t, half).start()
 
     def remap(t):
         def chunk(g, carry):
@@ -325,8 +347,8 @@
         lax.fori_loop(0, BLOCKS // 16, chunk, 0)
 
     def finish(t):
-        for half in range(2):
-            halo(t, half).wait_recv()
+        for q in range(LEVS // 2):
+            halo(t, q).wait_recv()
         remap(t)
 
     keep_main.wait()
@@ -343,12 +365,14 @@
             gather_sum(TRACERS - 1, half_of(s))
         if 0 < s < TRACERS:
             finish(s - 1)
+        if s == TRACERS - 2:
+            add_extras(TRACERS - 1)
     finish(TRACERS - 1)
     for s in range(2, PHASES):
         wait_bytes(sbuf, s, send_sem.at[s])
     for t in range(TRACERS):
-        for half in range(2):
-            halo(t, half).wait_send()
+        for q in range(LEVS // 2):
+            halo(t, q).wait_send()
     for n in range(4):
         for way in (1, -1):
             ring(n, way).wait_send()
@@ -357,16 +381,18 @@
 
 def on_device(tracers, sweeps, targets, matrix_ids, self_ids, vertical):
     vmem = pl.BlockSpec(memory_space=pltpu.VMEM)
-    smem = pl.BlockSpec(memory_space=pltpu.SMEM)
     hbm = pl.BlockSpec(memory_space=pl.ANY)
     dma = pltpu.SemaphoreType.DMA
     return pl.pallas_call(
         main_kernel,
         name="remap",
         out_shape=pltpu.VMEM((BLOCKS, TRACERS, LEVS, CELLS), bf16),
-        in_specs=[vmem, vmem, smem, hbm, hbm, hbm],
+        in_specs=[hbm] * 6,
         out_specs=vmem,
         scratch_shapes=[
+            pltpu.VMEM((3, BLOCKS), i32),
+            pltpu.VMEM((3, 2, BLOCKS), i32),
+            pltpu.SMEM((2, BLOCKS), i32),
             pltpu.VMEM((BLOCKS, ROWS, CELLS), bf16),
             pltpu.VMEM((32, CELLS, CELLS), bf16),
             pltpu.VMEM((TAP * LEVS, BLOCKS), f32),
@@ -384,8 +410,8 @@
             pltpu.VMEM((BLOCKS, 128), f32),
             pltpu.VMEM((TAP * LEVS, BLOCKS, CELLS), f32),
             pltpu.VMEM((16 * LEVS, CELLS), f32),
-            dma((4,)), dma((PHASES,)), dma((PHASES,)), dma((2, 4)), dma((2, 4)), dma((4,)), dma((4,)),
-            dma((2, TRACERS)), dma((2, TRACERS)), dma((2,)),
+            dma((7,)), dma((PHASES,)), dma((PHASES,)), dma((2, 4)), dma((2, 4)), dma((4,)), dma((4,)),
+            dma((LEVS // 2, TRACERS)), dma((LEVS // 2, TRACERS)), dma((2,)),
         ],
         compiler_params=pltpu.CompilerParams(
             collective_id=0, has_side_effects=True, vmem_limit_bytes=56 * 1024 * 1024

time: 169 us -> 168 us (level)
  Pallas kernels: 168 us -> 166 us
where the time goes in v5:
time: 168 us
  Pallas kernels  166 us (99%)
    pallas_call x1, Pallas kernels, on_device(): pl.pallas_call(main_kernel, name='remap', out_shape=pltpu.VMEM((BLOCKS, T...  166 us

profile of v5, /device:TPU:1, one launch (start us, length us, event | category | flops | bytes accessed | tf_op | source)
XLA Modules:
  0.0 167.8 jit_solution(12129854551491694487)
XLA Ops:
  0.0 166.5 %remap.1 = bf16[256,4,8,128]{3,2,1,0:T(8,128)(2,1)S(1)} custom-call(s32[3,256]{1,0:T(4,128)} %bitcast.10, s32[3,2,256]{2,1,0:T(2,128)} %bitcast.9, s32[2,256]{1,0:T(2,128)} %bitcast.11, bf16[256,32,128]{2,1,0:T(8,128)(2,1)} %bitcast.6, bf16[32,128,128]{2,1,0:T(8,128)(2,1)} %bitcast.7, f32[72,256]{1,0:T(8,128)} %bitcast.8), custom_call_target="tpu_custom_call" | custom-call | tf_op jit(solution)/shard_map/remap/pallas_call | solution.py:386
  166.5 1.3 copy.8

commit v6 on v5

--- a/solution.py
+++ b/solution.py
@@ -41,7 +41,7 @@
     target_in, matrix_in, self_in, tracers_in, sweeps_in, vertical_in, out_ref,
     target_ref, matrix_ref, self_ref,
     tracers_ref, sweeps_ref, vertical_ref, table_made, table_ref, head, hot,
-    stage, sbuf, rbuf, ebuf, own, chosen, pad, turned, weight, turn,
+    stage, sbuf, rbuf, ebuf, own, chosen, pad, turned, weight, turn, late,
     in_sem, send_sem, recv_sem, ring_send, ring_recv, cross_send, cross_recv, halo_send, halo_recv, local_sem,
 ):
     me = lax.axis_index("tile")
@@ -346,6 +346,31 @@
 
         lax.fori_loop(0, BLOCKS // 16, chunk, 0)
 
+    def remap_half(half, last):
+        t = TRACERS - 1
+
+        def chunk(g, carry):
+            rows = pl.ds(pl.multiple_of(g * 16, 16), 16)
+            levels = [pad[t, REACH * half + m, rows].astype(f32) for m in range(REACH + 2 * REACH)]
+            for l in range(REACH):
+                total = weight[REACH * half + l, rows] * levels[l]
+                for n in range(1, TAP):
+                    total = total + weight[n * LEVS + REACH * half + l, rows] * levels[l + n]
+                late[pl.ds(g * 16 * LEVS + REACH * half + l, 16, stride=LEVS), :] = total
+            if last:
+                for b in range(16):
+                    tile = late[pl.ds(pl.multiple_of((g * 16 + b) * LEVS, 8), LEVS), :]
+                    out_ref[g * 16 + b, t] = tile.astype(bf16)
+            return carry
+
+        lax.fori_loop(0, BLOCKS // 16, chunk, 0)
+
+    def finish_last():
+        for half, last in ((first_half, False), (1 - first_half, True)):
+            for n in range(2):
+                halo(TRACERS - 1, 2 * (1 - half) + n).wait_recv()
+            remap_half(half, last)
+
     def finish(t):
         for q in range(LEVS // 2):
             halo(t, q).wait_recv()
@@ -367,7 +392,7 @@
             finish(s - 1)
         if s == TRACERS - 2:
             add_extras(TRACERS - 1)
-    finish(TRACERS - 1)
+    finish_last()
     for s in range(2, PHASES):
         wait_bytes(sbuf, s, send_sem.at[s])
     for t in range(TRACERS):
@@ -410,6 +435,7 @@
             pltpu.VMEM((BLOCKS, 128), f32),
             pltpu.VMEM((TAP * LEVS, BLOCKS, CELLS), f32),
             pltpu.VMEM((16 * LEVS, CELLS), f32),
+            pltpu.VMEM((BLOCKS * LEVS, CELLS), f32),
             dma((7,)), dma((PHASES,)), dma((PHASES,)), dma((2, 4)), dma((2, 4)), dma((4,)), dma((4,)),
             dma((LEVS // 2, TRACERS)), dma((LEVS // 2, TRACERS)), dma((2,)),
         ],

time: 168 us -> 168 us (level)
  no operation moved by 1% of the time
where the time goes in v6:
time: 168 us; the launch traced here: 167 us
  Pallas kernels  166 us (99%)
    pallas_call x1, Pallas kernels, on_device(): pl.pallas_call(main_kernel, name='remap', out_shape=pltpu.VMEM((BLOCKS, T...  166 us

profile of v6, /device:TPU:1, one launch (start us, length us, event | category | flops | bytes accessed | tf_op | source)
XLA Modules:
  0.0 167.4 jit_solution(15084543488348496038)
XLA Ops:
  0.0 166.1 %remap.1 = bf16[256,4,8,128]{3,2,1,0:T(8,128)(2,1)S(1)} custom-call(s32[3,256]{1,0:T(4,128)} %bitcast.10, s32[3,2,256]{2,1,0:T(2,128)} %bitcast.9, s32[2,256]{1,0:T(2,128)} %bitcast.11, bf16[256,32,128]{2,1,0:T(8,128)(2,1)} %bitcast.6, bf16[32,128,128]{2,1,0:T(8,128)(2,1)} %bitcast.7, f32[72,256]{1,0:T(8,128)} %bitcast.8), custom_call_target="tpu_custom_call" | custom-call | tf_op jit(solution)/shard_map/remap/pallas_call | solution.py:411
  166.1 1.3 copy.8
